TPU v7x, 32 devices: a whole 2x2x4 slice. The times are simulated.
32 devices in a mesh: dp: 8 (over z, x), tensor: 4 (over y, core).
Axes of the slice: x: 2, y: 2, z: 4, core: 2. Of those that a mesh axis runs over, the one named last changes fastest.
Arguments:
- block_input: bfloat16 [16, 1024, 1536], P('dp', 'tensor'), may hold values from -6 to 6
- out_grad: bfloat16 [16, 1024, 1536], P('dp', 'tensor'), may hold values from -6 to 6
- seg_lengths: int32 [16, 4], P('dp'), may hold values from 1 to 1020, as said below
- norm1_gain: bfloat16 [1536], replicated, may hold values from 0.5 to 1.5
- norm2_gain: bfloat16 [1536], replicated, may hold values from 0.5 to 1.5
- rel_bias: bfloat16 [32, 12], replicated, may hold values from -3 to 3
- w_query: bfloat16 [1536, 768], P(None, 'tensor'), may hold values from -0.078125 to 0.078125
- w_key: bfloat16 [1536, 768], P(None, 'tensor'), may hold values from -0.078125 to 0.078125
- w_value: bfloat16 [1536, 768], P(None, 'tensor'), may hold values from -0.15625 to 0.15625
- w_out: bfloat16 [768, 1536], P('tensor'), may hold values from -0.75 to 0.75
- w_gate: bfloat16 [1536, 3968], P(None, 'tensor'), may hold values from -0.15625 to 0.15625
- w_up: bfloat16 [1536, 3968], P(None, 'tensor'), may hold values from -0.15625 to 0.15625
- w_down: bfloat16 [3968, 1536], P('tensor'), may hold values from -0.09375 to 0.09375
Outputs:
- block_out: float32 [16, 1024, 1536], P('dp', 'tensor')
- input_grad: float32 [16, 1024, 1536], P('dp', 'tensor')
- norm1_grad: float32 [1536], replicated
- norm2_grad: float32 [1536], replicated
- bias_grad: float32 [32, 12], replicated
- query_grad: float32 [1536, 768], P('dp', 'tensor')
- key_grad: float32 [1536, 768], P('dp', 'tensor')
- value_grad: float32 [1536, 768], P('dp', 'tensor')
- outproj_grad: float32 [768, 1536], P('tensor', 'dp')
- gate_grad: float32 [1536, 3968], P('dp', 'tensor')
- up_grad: float32 [1536, 3968], P('dp', 'tensor')
- down_grad: float32 [3968, 1536], P('tensor', 'dp')
Inputs may be any that keep to these rules, and one draw needn't show every extreme that they name: `seg_lengths`: each row's 4 lengths add up to less than 1024; the remaining positions of the row are padding. In every row one segment covers more than three quarters of the row. In some row of every draw the longest segment has exactly 1020 positions.
All inputs are finite; a program needn't handle non-finite values.
Results may differ from a plain program's by a relative error of at most 0.014.
The roundings to bfloat16 on the way count: a program that leaves them out, or rounds other values in their place, can miss the bound.
Values may be sent and summed in bfloat16 or wider, within the bound.
No kernel may reach another device: no remote copies, remote signals or barrier semaphores. Data moves between devices by JAX's collectives and lax.ppermute only.
A program may use at most 256 MiB of HBM per device.

v0:
```python
import functools

import jax
import jax.numpy as jnp
import numpy as np
from jax import lax
from jax.experimental import pallas as pl
from jax.experimental.pallas import tpu as pltpu
from jax.sharding import PartitionSpec as P

DK = 64
QUERY_BLOCK = 256
REACH = 128
LANES = 64
MIB = 2**20

bucket_edges = (12, 16, 23, 32, 46, 64, 91)
masked_score = -1000000000.0
epsilon = 1e-06
gelu_scale = float(np.sqrt(2 / np.pi))
gelu_cubic = 0.044715
bf16 = jnp.bfloat16
f32 = jnp.float32

across_y = ((0, 2), (2, 0), (1, 3), (3, 1))
across_core = ((0, 1), (1, 0), (2, 3), (3, 2))
across_both = ((0, 3), (3, 0), (1, 2), (2, 1))


def dot_nn(left, right):
    return lax.dot_general(left, right, (((1,), (0,)), ((), ())), preferred_element_type=f32)


def dot_nt(left, right):
    return lax.dot_general(left, right, (((1,), (1,)), ((), ())), preferred_element_type=f32)


def dot_tn(left, right):
    return lax.dot_general(left, right, (((0,), (0,)), ((), ())), preferred_element_type=f32)


def over_y(array):
    return lax.ppermute(array, "tensor", across_y)


def over_core(array):
    return lax.ppermute(array, "tensor", across_core)


def over_both(array):
    return lax.ppermute(array, "tensor", across_both)


smem = pl.BlockSpec(memory_space=pltpu.SMEM)
vmem = pl.BlockSpec(memory_space=pltpu.VMEM)
anywhere = pl.BlockSpec(memory_space=pl.ANY)


def piece_of(array, lead):
    return vmem if lead is None else row_of(lead, array.shape)


def row_of(row, shape):
    return pl.BlockSpec((1,) + shape[1:], lambda *_: (row, 0, 0))


def placed(shape, kind, space=None):
    return jax.ShapeDtypeStruct(shape, kind) if space is None else space(shape, kind)


class Order:
    def __init__(self):
        self.last = []

    def after(self, *arrays):
        self.last = self.last + list(arrays)

    def call(self, kernel, name, inputs, in_specs, outputs, room, scratch=(), out_specs=None, grid=(1,), aliases=None):
        count, extra = len(inputs), len(self.last)

        def body(*refs):
            kernel(*refs[:count], *refs[count + extra :])

        results = pl.pallas_call(
            body,
            grid=grid,
            in_specs=list(in_specs) + [anywhere] * extra,
            out_specs=out_specs or [vmem] * len(outputs),
            out_shape=[placed(*output) for output in outputs],
            scratch_shapes=scratch,
            input_output_aliases=aliases or {},
            compiler_params=pltpu.CompilerParams(vmem_limit_bytes=room * MIB),
            cost_estimate=pl.CostEstimate(flops=10**13, bytes_accessed=1024, transcendentals=0),
            name=name,
        )(*inputs, *self.last)
        self.last = [results[0]]
        return results


def norm_factor(rows):
    return lax.rsqrt(jnp.mean(rows * rows, axis=-1, keepdims=True) + epsilon)


def norm_backward(dnormed, rows, gain):
    factor = norm_factor(rows)
    scaled = dnormed * gain
    return factor * (scaled - rows * factor * factor * jnp.mean(scaled * rows, axis=-1, keepdims=True))


def project_kernel(own, other_y, other_core, other_both, gain, weight_t, normed, qkv):
    count = own.shape[1]
    for index, piece in enumerate((own, other_y, other_core, other_both)):
        rows = piece[...].reshape(own.shape[1:]).astype(f32)
        result = (rows * norm_factor(rows) * gain[...]).astype(bf16)
        at = slice(index * count, (index + 1) * count)
        normed[at, :] = result
        qkv[at, :] = dot_nt(result, weight_t[...]).astype(bf16)


def project(order, pieces, gain, weight_t):
    count, width = pieces[0][0].shape[1:]
    return order.call(
        project_kernel,
        "normed_projections",
        (*[array for array, _ in pieces], gain, weight_t),
        [piece_of(*piece) for piece in pieces] + [vmem, vmem],
        [((4 * count, width), bf16), ((4 * count, weight_t.shape[0]), bf16)],
        36,
    )


def bucket_of(offset, buckets):
    magnitude = jnp.abs(offset)
    larger = sum(((magnitude >= edge).astype(jnp.int32) for edge in bucket_edges))
    exact = buckets // 4
    inside = jnp.where(magnitude < exact, magnitude, exact + larger)
    return inside + jnp.where(offset > 0, buckets // 2, 0)


def band_buckets(buckets):
    key = jnp.arange(QUERY_BLOCK + 2 * REACH, dtype=jnp.int32) - REACH
    query = jnp.arange(QUERY_BLOCK, dtype=jnp.int32)
    return bucket_of(key[:, None] - query[None, :], buckets)


def bias_parts(bias, length):
    buckets = bias.shape[0]
    index = band_buckets(buckets)
    wide = bias.astype(f32)
    band = jnp.zeros((bias.shape[1],) + index.shape, f32)
    for bucket in range(buckets):
        band = jnp.where((index == bucket)[None], wide[bucket][:, None, None], band)
    key = jnp.arange(length, dtype=jnp.int32)[:, None]
    block = jnp.arange(LANES, dtype=jnp.int32)[None]
    used = block < length // QUERY_BLOCK
    before = (key < block * QUERY_BLOCK - REACH) & used
    after = (key >= (block + 1) * QUERY_BLOCK + REACH) & used
    far_before = bias[buckets // 2 - 1][:, None, None]
    far_after = bias[buckets - 1][:, None, None]
    far = jnp.where(before[None], far_before, jnp.where(after[None], far_after, jnp.zeros((), bias.dtype)))
    return band, far


def near_keys(block, length):
    low = max(0, block * QUERY_BLOCK - REACH)
    high = min(length, (block + 1) * QUERY_BLOCK + REACH)
    return low, high, low - (block * QUERY_BLOCK - REACH)


def segment_of(position, lengths, row):
    end = jnp.int32(0)
    segment = jnp.zeros(position.shape, jnp.int32)
    for part in range(lengths.shape[1]):
        end = end + lengths[row, part]
        segment = segment + (position >= end).astype(jnp.int32)
    return segment


def fill_masks(lengths, row, masks):
    blocks, length, width = masks.shape
    key_segment = segment_of(lax.broadcasted_iota(jnp.int32, (length, width), 0), lengths, row)
    for block in range(blocks):
        at = lax.broadcasted_iota(jnp.int32, (1, width), 1) + block * width
        masks[block] = jnp.where(key_segment == segment_of(at, lengths, row), 0.0, masked_score)


def relative_block(place, block):
    along_y = jnp.bitwise_xor(place[0], block // 2)
    along_core = jnp.bitwise_xor(place[1], block % 2)
    return along_y + 2 * along_core


def rows_at(index):
    return pl.ds(pl.multiple_of(index * QUERY_BLOCK, QUERY_BLOCK), QUERY_BLOCK)


def block_scores(key_wide, query_wide, mask, band, head, block):
    length = key_wide.shape[0]
    scores = dot_nt(key_wide, query_wide) + mask
    low, high, start = near_keys(block, length)
    parts = []
    if low > 0:
        parts.append(scores[:low])
    parts.append(scores[low:high] + band[head, start : start + high - low])
    if high < length:
        parts.append(scores[high:])
    return jnp.concatenate(parts, axis=0)


def block_indicator(block):
    lane = lax.broadcasted_iota(jnp.int32, (QUERY_BLOCK, LANES), 1)
    return jnp.where(lane == block, 1.0, 0.0).astype(bf16)


def attention_forward_kernel(
    row, place, lengths, qkv, band, far, attended_keep, attended_send, logsum, masks, keys, values, attended
):
    length = qkv.shape[0]
    width = qkv.shape[1] // 3
    fill_masks(lengths, row, masks)
    blocks = length // QUERY_BLOCK
    order = [relative_block(place, block) for block in range(blocks)]
    for block in range(blocks):
        at = slice(block * QUERY_BLOCK, (block + 1) * QUERY_BLOCK)
        keys[at, :] = qkv[rows_at(order[block]), width : 2 * width]
        values[at, :] = qkv[rows_at(order[block]), 2 * width :]
    for head in range(width // DK):
        cols = slice(head * DK, (head + 1) * DK)
        key_wide = jnp.concatenate([keys[:, cols], far[head]], axis=1)
        for block in range(blocks):
            query_wide = jnp.concatenate([qkv[rows_at(order[block]), cols], block_indicator(block)], axis=1)
            scores = block_scores(key_wide, query_wide, masks[block], band, head, block)
            peak = jnp.max(scores, axis=0, keepdims=True)
            expo = jnp.exp(scores - peak)
            total = jnp.sum(expo, axis=0, keepdims=True)
            probs_low = (expo * (1.0 / total)).astype(bf16)
            logsum[head : head + 1, block * QUERY_BLOCK : (block + 1) * QUERY_BLOCK] = peak + jnp.log(total)
            result = dot_tn(probs_low, values[:, cols]).astype(bf16)
            attended[rows_at(order[block]), cols] = result
    attended_keep[...] = attended[: length // 2, :]
    attended_send[...] = attended[length // 2 :, :]


def attention_forward(order, row, place, lengths, qkv, band, far):
    length, width = qkv.shape[0], qkv.shape[1] // 3
    return order.call(
        functools.partial(attention_forward_kernel, row),
        "attention_forward",
        (place, lengths, qkv, band, far),
        [smem, smem, vmem, vmem, vmem],
        [((length // 2, width), bf16), ((length // 2, width), bf16), ((8, length), f32)],
        36,
        scratch=[
            pltpu.VMEM((length // QUERY_BLOCK, length, QUERY_BLOCK), f32),
            pltpu.VMEM((length, width), bf16),
            pltpu.VMEM((length, width), bf16),
            pltpu.VMEM((length, width), bf16),
        ],
    )


def attention_backward_kernel(
    row, place, lengths, qkv, dout_own, dout_y, dout_core, logsum, band, far, weight_t, normed,
    dqkv, dnormed_keep, dnormed_send, band_grad, far_grad, gain_sum,
    masks, keys, values, douts, queries_wide, probs_low, dscores,
):
    length = qkv.shape[0]
    width = qkv.shape[1] // 3
    fill_masks(lengths, row, masks)
    blocks = length // QUERY_BLOCK
    order = [relative_block(place, block) for block in range(blocks)]
    for block, piece in enumerate((dout_own[...], dout_y[0], dout_core[0], dout_core[1])):
        at = slice(block * QUERY_BLOCK, (block + 1) * QUERY_BLOCK)
        keys[at, :] = qkv[rows_at(order[block]), width : 2 * width]
        values[at, :] = qkv[rows_at(order[block]), 2 * width :]
        true_block = 2 * jnp.bitwise_xor(place[0], block % 2) + jnp.bitwise_xor(place[1], block // 2)
        douts[rows_at(true_block), :] = piece
    band_grad[...] = jnp.zeros_like(band_grad)
    far_grad[...] = jnp.zeros_like(far_grad)
    key_at = lax.broadcasted_iota(jnp.int32, (length, LANES), 0)
    block_at = lax.broadcasted_iota(jnp.int32, (length, LANES), 1)
    before = key_at < block_at * QUERY_BLOCK - REACH
    after = key_at >= (block_at + 1) * QUERY_BLOCK + REACH
    for head in range(width // DK):
        cols = slice(head * DK, (head + 1) * DK)
        slot = head % 2
        key_head = keys[:, cols]
        key_wide = jnp.concatenate([key_head, far[head]], axis=1)
        value_head = values[:, cols]
        for block in range(blocks):
            at = slice(block * QUERY_BLOCK, (block + 1) * QUERY_BLOCK)
            query_wide = jnp.concatenate([qkv[rows_at(order[block]), cols], block_indicator(block)], axis=1)
            queries_wide[slot, at, :] = query_wide
            scores = block_scores(key_wide, query_wide, masks[block], band, head, block)
            probs = jnp.exp(scores - logsum[head : head + 1, at])
            weighted = probs * dot_nt(value_head, douts[at, cols])
            inner = jnp.sum(weighted, axis=0, keepdims=True)
            low_dscores = (weighted - probs * inner).astype(bf16)
            probs_low[slot, :, at] = probs.astype(bf16)
            dscores[slot, :, at] = low_dscores
            low, high, start = near_keys(block, length)
            band_grad[head, start : start + high - low] += low_dscores[low:high].astype(f32)
        dvalue = dot_nn(probs_low[slot], douts[:, cols])
        dkey_wide = dot_nn(dscores[slot], queries_wide[slot])
        dquery = dot_nn(key_head.T, dscores[slot]).T
        for block in range(blocks):
            at = slice(block * QUERY_BLOCK, (block + 1) * QUERY_BLOCK)
            for index, part in enumerate((dquery, dkey_wide[:, :DK], dvalue)):
                part_cols = slice(index * width + head * DK, index * width + (head + 1) * DK)
                dqkv[rows_at(order[block]), part_cols] = part[at].astype(bf16)
        sums = dkey_wide[:, DK:]
        far_grad[head : head + 1, :] += jnp.concatenate(
            [
                jnp.sum(jnp.where(before, sums, 0.0), axis=0, keepdims=True),
                jnp.sum(jnp.where(after, sums, 0.0), axis=0, keepdims=True),
            ],
            axis=1,
        )
    total = jnp.zeros((1, normed.shape[1]), f32)
    for half, target in enumerate((dnormed_keep, dnormed_send)):
        for part in range(2):
            at = slice((2 * half + part) * QUERY_BLOCK, (2 * half + part + 1) * QUERY_BLOCK)
            dnormed = dot_nn(dqkv[at, :], weight_t[...])
            target[part * QUERY_BLOCK : (part + 1) * QUERY_BLOCK, :] = dnormed.astype(bf16)
            total = total + jnp.sum(dnormed * normed[at, :].astype(f32), axis=0, keepdims=True)
    gain_sum[...] = total


def attention_backward(order, row, place, lengths, qkv, douts, logsum, band, far, weight_t, normed):
    length, width = qkv.shape[0], qkv.shape[1] // 3
    half = ((length // 2, normed.shape[1]), bf16)
    return order.call(
        functools.partial(attention_backward_kernel, row),
        "attention_backward",
        (place, lengths, qkv, *douts, logsum, band, far, weight_t, normed),
        [smem, smem] + [vmem] * 9,
        [(qkv.shape, bf16, pltpu.HBM), half, half, (band.shape, f32), ((8, 2 * LANES), f32)]
        + [((1, normed.shape[1]), f32)],
        52,
        scratch=[pltpu.VMEM((length // QUERY_BLOCK, length, QUERY_BLOCK), f32)]
        + [pltpu.VMEM((length, width), bf16)] * 3
        + [pltpu.VMEM((2, length, DK + LANES), bf16)]
        + [pltpu.VMEM((2, length, length), bf16)] * 2,
    )


def branch_kernel(heads_0, heads_1, heads_2, heads_3, out_0, out_1, out_2, out_3, own, other_y, gain, middle, normed):
    count = own.shape[1]
    for index, piece in enumerate((own, other_y)):
        here = slice(index * count, (index + 1) * count)
        there = slice((1 - index) * count, (2 - index) * count)
        branch = (
            dot_nn(heads_0[here, :], out_0[...])
            + dot_nn(heads_1[here, :], out_1[...])
            + dot_nn(heads_2[there, :], out_2[...])
            + dot_nn(heads_3[there, :], out_3[...])
        )
        rows = piece[...].reshape(branch.shape).astype(f32) + branch
        if index == 0:
            middle[...] = rows
        normed[here, :] = (rows * norm_factor(rows) * gain[...]).astype(bf16)


def attention_branch(order, heads, out_parts, own, other_y, gain):
    count, width = own[0].shape[1:]
    return order.call(
        branch_kernel,
        "attention_branch",
        (*heads, *out_parts, own[0], other_y[0], gain),
        [vmem] * 8 + [piece_of(*own), piece_of(*other_y), vmem],
        [((count, width), f32), ((2 * count, width), bf16)],
        28,
    )


def branch_backward_kernel(
    keep, received, from_y, middle, out_grad, gain, out_0, out_1, out_2, out_3,
    dmiddle, dbranch, gain_sum, douts_own, douts_core, douts_y,
):
    dnormed = summed(keep, received, from_y)
    rows = middle[...]
    result = out_grad[0].astype(f32) + norm_backward(dnormed, rows, gain[...])
    dmiddle[...] = result
    low = result.astype(bf16)
    dbranch[...] = low
    gain_sum[...] = jnp.sum(dnormed * rows * norm_factor(rows), axis=0, keepdims=True)
    douts_own[...] = dot_nt(low, out_0[...]).astype(bf16)
    douts_core[...] = dot_nt(low, out_1[...]).astype(bf16)
    douts_y[0] = dot_nt(low, out_2[...]).astype(bf16)
    douts_y[1] = dot_nt(low, out_3[...]).astype(bf16)


def branch_backward(order, row, keep, received, from_y, middle, out_grad, gain, out_parts):
    count, width = middle.shape
    first = pl.BlockSpec((count, width), lambda *_: (0, 0))
    return order.call(
        branch_backward_kernel,
        "branch_backward",
        (keep, received, from_y, middle, out_grad, gain, *out_parts),
        [first, pl.BlockSpec((1, count, width), lambda *_: (0, 0, 0)), vmem, vmem, row_of(row, out_grad.shape)]
        + [vmem] * 5,
        [((count, width), f32), ((count, width), bf16), ((1, width), f32)]
        + [((count, out_parts[0].shape[0]), bf16)] * 2
        + [((2, count, out_parts[0].shape[0]), bf16)],
        24,
    )


def outproj_grad_kernel(rows, *refs):
    heads, branches, (keep, send) = refs[: 4 * rows], refs[4 * rows : 5 * rows], refs[5 * rows :]
    count = branches[0].shape[0]
    for index in range(4):
        total = None
        for row in range(rows):
            at = slice((index // 2) * count, (index // 2 + 1) * count)
            part = dot_tn(heads[4 * row + index][at, :], branches[row][...])
            total = part if total is None else total + part
        target = keep if index % 2 == 0 else send
        target[index // 2] = total.astype(bf16)


def outproj_grad(order, heads, branches):
    rows, width, cols = len(branches), branches[0].shape[1], heads[0].shape[1]
    return order.call(
        functools.partial(outproj_grad_kernel, rows),
        "outproj_gradient",
        (*heads, *branches),
        [vmem] * (5 * rows),
        [((2, cols, width), bf16)] * 2,
        24,
    )


def feed_kernel(chunk, blocks, leads, normed_keep, normed_recv, *refs):
    count = len(blocks)
    grads_hbm, (gate_hbm, up_hbm, down_hbm), refs = refs[:count], refs[count : count + 3], refs[count + 3 :]
    refs = refs[-12:]
    hidden_ref, dgate_ref, dup_ref, dnormed_keep, feed_keep, sends = refs[:6]
    gate_t, up_t, down, grads, weight_sem, grad_sem = refs[6:]
    step = pl.program_id(0)
    units = down.shape[0]
    chunks = [slice(start, min(units, start + chunk)) for start in range(0, units, chunk)]
    kept = sum(block < 2 for block in blocks)

    def weight_copies(index):
        at = pl.ds(chunks[index].start, chunks[index].stop - chunks[index].start)
        pairs = ((gate_hbm, gate_t), (up_hbm, up_t), (down_hbm, down))
        return [
            pltpu.make_async_copy(source.at[at], target.at[at], weight_sem.at[index, which])
            for which, (source, target) in enumerate(pairs)
        ]

    def grad_copy(index):
        source = grads_hbm[index] if leads[index] is None else grads_hbm[index].at[leads[index]]
        return pltpu.make_async_copy(source, grads.at[index], grad_sem.at[index])

    def work(first):
        normed = jnp.where(step < kept, normed_keep[...], normed_recv[...])
        grad = grads[step]
        for index, at in enumerate(chunks):
            if first:
                for copy in weight_copies(index):
                    copy.wait()
            values = gated_products(normed, grad, gate_t[at, :], up_t[at, :], down[at, :])
            hidden_ref[:, at], dgate_ref[:, at], dup_ref[:, at] = values
        for ref in (dgate_ref, dup_ref):
            ref[:, units:] = jnp.zeros((ref.shape[0], ref.shape[1] - units), bf16)
        dnormed = dot_nn(dgate_ref[:, :units], gate_t[...]) + dot_nn(dup_ref[:, :units], up_t[...])
        dnormed = dnormed.astype(bf16)
        feed = dot_nn(hidden_ref[...], down[...]).astype(bf16)

        @pl.when(step < kept)
        def _():
            dnormed_keep[...] = dnormed
            feed_keep[...] = feed

        @pl.when(step >= kept)
        def _():
            sends[0] = dnormed
            sends[1] = feed

    @pl.when(step == 0)
    def _():
        for index in range(len(chunks)):
            for copy in weight_copies(index):
                copy.start()
            if index == 0:
                grad_copy(0).start()
        for index in range(1, count):
            grad_copy(index).start()
        grad_copy(0).wait()
        work(True)

    @pl.when(step > 0)
    def _():
        for index in range(1, count):
            pl.when(step == index)(grad_copy(index).wait)
        work(False)


def feed_forward(order, normed_keep, normed_recv, blocks, grads, gate_t, up_t, down, before=()):
    units, width = down.shape
    length = 2 * normed_keep.shape[0]
    count = length // 4
    if len(blocks) == 4:
        kept_at, sent_at, at = (lambda s: jnp.minimum(s, 1)), (lambda s: jnp.maximum(s - 2, 0)), (lambda s: s)
    else:
        low, high = blocks
        kept_at = sent_at = lambda s: low
        at = lambda s: low + s * (high - low)
    first = pl.BlockSpec((count, width), lambda step: (kept_at(step), 0))
    last = pl.BlockSpec((count, width), lambda step: (sent_at(step), 0))
    pair = pl.BlockSpec((2, count, width), lambda step: (0, sent_at(step), 0))
    each = pl.BlockSpec((count, units), lambda step: (at(step), 0))
    wide = -(-units // 128) * 128
    padded = pl.BlockSpec((count, wide), lambda step: (at(step), 0))
    half = ((length // 2, width), bf16)
    chunk = 256
    inputs = 5 + len(grads)
    return order.call(
        functools.partial(feed_kernel, chunk, blocks, [lead for _, lead in grads]),
        "feed_forward",
        (normed_keep, normed_recv, *[array for array, _ in grads], gate_t, up_t, down, *before),
        [first, last] + [anywhere] * (inputs - 2 + len(before)),
        [((length, units), bf16, pltpu.HBM)]
        + [((length, wide), bf16, pltpu.HBM)] * 2
        + [half, half, ((2, length // 2, width), bf16)],
        44,
        out_specs=[each, padded, padded, first, first, pair],
        grid=(len(blocks),),
        scratch=[pltpu.VMEM((units, width), bf16)] * 3
        + [
            pltpu.VMEM((len(blocks), count, width), bf16),
            pltpu.SemaphoreType.DMA((-(-units // chunk), 3)),
            pltpu.SemaphoreType.DMA((len(blocks),)),
        ],
        aliases={inputs + index: index for index in range(len(before))},
    )


def gated_products(normed, grad, gate, up, down):
    gate = dot_nt(normed, gate)
    up = dot_nt(normed, up)
    dhidden = dot_nt(grad, down)
    square = gate * gate
    bend = jnp.tanh(gelu_scale * gate * (1.0 + gelu_cubic * square))
    half = 0.5 * (1.0 + bend)
    active = gate * half
    slope = half + (0.5 * gelu_scale) * gate * (1.0 - bend * bend) * (1.0 + (3 * gelu_cubic) * square)
    return (active * up).astype(bf16), (dhidden * up * slope).astype(bf16), (dhidden * active).astype(bf16)


def feed_last_kernel(chunk, pieces, rows, bits, place, *refs):
    count = sum(map(len, pieces))
    arrays, refs = refs[:count], refs[count:]
    earlier, refs = refs[: 3 * (rows - 1)], refs[3 * (rows - 1) :]
    (gate_hbm, up_hbm, down_hbm), refs = refs[:3], refs[3:]
    (dnormed_keep, feed_keep, sends), outs, refs = refs[:3], refs[3:9], refs[9:]
    gate_t, up_t, down, normed, grads, hidden, dgate, dup, stage = refs[:9]
    weight_sem, left_sem, right_sem, out_sem = refs[9:]
    step = pl.program_id(0)
    units = down.shape[0]
    chunks = [slice(start, min(units, start + chunk)) for start in range(0, units, chunk)]
    length = normed.shape[0] // rows
    block = length // 4
    base = (rows - 1) * length

    def weight_copies(index):
        at = pl.ds(chunks[index].start, chunks[index].stop - chunks[index].start)
        pairs = ((gate_hbm, gate_t), (up_hbm, up_t), (down_hbm, down))
        return [
            pltpu.make_async_copy(source.at[at], target.at[at], weight_sem.at[index, which])
            for which, (source, target) in enumerate(pairs)
        ]

    def left_copies(side):
        copies = []
        taken = sum(map(len, pieces[:side]))
        at = 0
        for index, lead in enumerate(pieces[side]):
            source = arrays[taken + index]
            source = source if lead is None else source.at[lead]
            copies.append(
                (
                    at,
                    pltpu.make_async_copy(
                        source, (normed, grads)[side].at[pl.ds(at, source.shape[0])], left_sem.at[side, index]
                    ),
                )
            )
            at += source.shape[0]
        return copies

    def right_copies():
        return [
            pltpu.make_async_copy(
                earlier[3 * row + which], target.at[pl.ds(row * length, length)], right_sem.at[row, which]
            )
            for row in range(rows - 1)
            for which, target in enumerate((hidden, dgate, dup))
        ]

    def work(first):
        at = pl.ds(pl.multiple_of(base + step * block, block), block)
        rows_normed, rows_grad = normed[at, :], grads[at, :]
        for index, part in enumerate(chunks):
            if first:
                for copy in weight_copies(index):
                    copy.wait()
            values = gated_products(rows_normed, rows_grad, gate_t[part, :], up_t[part, :], down[part, :])
            for target, value in zip((hidden, dgate, dup), values):
                target[at, part] = value
        dnormed = dot_nn(dgate[at, :units], gate_t[...]) + dot_nn(dup[at, :units], up_t[...])
        dnormed = dnormed.astype(bf16)
        feed = dot_nn(hidden[at, :], down[...]).astype(bf16)

        @pl.when(step < 2)
        def _():
            dnormed_keep[...] = dnormed
            feed_keep[...] = feed

        @pl.when(step >= 2)
        def _():
            sends[0] = dnormed
            sends[1] = feed

    def gradients():
        width = normed.shape[1]
        chunk_rows = outs[0].shape[1]
        tile = width // 2
        half_rows = tile // 2
        half_chunks = half_rows // chunk_rows
        sending = {}
        turn = 0
        for product, (left, right) in enumerate(((grads, hidden), (normed, dgate), (normed, dup))):
            bit = bits[product]
            for part in range(2):
                slot = turn % 2
                turn += 1
                for copy in sending.get(slot, ()):
                    copy.wait()
                for half in range(2):
                    cols = slice(part * tile + half * half_rows, part * tile + (half + 1) * half_rows)
                    value = dot_tn(left[:, cols], right[:, :units]).reshape(half_chunks, chunk_rows, units)
                    stage[slot, half * half_chunks : (half + 1) * half_chunks] = value.astype(bf16)
                sending[slot] = []
                for index in range(half_chunks):
                    low = index % (1 << bit)
                    first_chunk = (index - low) * 2 + low
                    for side, which in enumerate((place[2 + bit], 1 - place[2 + bit])):
                        copy = pltpu.make_async_copy(
                            stage.at[slot, first_chunk + which * (1 << bit)],
                            outs[2 * product + side].at[part * half_chunks + index],
                            out_sem.at[product, side, part * half_chunks + index],
                        )
                        copy.start()
                        sending[slot].append(copy)
        for copies in sending.values():
            for copy in copies:
                copy.wait()

    @pl.when(step == 0)
    def _():
        mine = [[copy for at, copy in left_copies(side) if at >= base] for side in range(2)]
        for index in range(len(chunks)):
            for copy in weight_copies(index):
                copy.start()
            if index == 0:
                mine[0][0].start()
                mine[1][0].start()
        for copies in mine:
            for copy in copies[1:]:
                copy.start()
        mine[0][0].wait()
        mine[1][0].wait()
        work(True)

    @pl.when(step == 1)
    def _():
        for side in range(2):
            for at, copy in left_copies(side):
                if at < base:
                    copy.start()
                elif at > base:
                    copy.wait()
        for copy in right_copies():
            copy.start()

    pl.when(step > 0)(lambda: work(False))

    @pl.when(step == 3)
    def _():
        for side in range(2):
            for at, copy in left_copies(side):
                if at < base:
                    copy.wait()
        for copy in right_copies():
            copy.wait()
        gradients()


def feed_last(order, place, lefts, earlier, gate_t, up_t, down, bits):
    units, width = down.shape
    size = lax.axis_size("dp")
    rows = len(earlier) + 1
    length = 4 * lefts[1][-1][0].shape[-2]
    count = length // 4
    first = pl.BlockSpec((count, width), lambda step: (jnp.minimum(step, 1), 0))
    pair = pl.BlockSpec((2, count, width), lambda step: (0, jnp.maximum(step - 2, 0), 0))
    half = ((length // 2, width), bf16)
    chunk = 256
    chunk_rows = width // size
    wide = -(-units // 128) * 128
    plan = [[lead for _, lead in side] for side in lefts]
    inputs = [array for side in lefts for array, _ in side] + [array for row in earlier for array in row]
    return order.call(
        functools.partial(feed_last_kernel, chunk, plan, rows, bits),
        "feed_forward_and_gradients",
        (place, *inputs, gate_t, up_t, down),
        [smem] + [anywhere] * (len(inputs) + 3),
        [half, half, ((2, length // 2, width), bf16)] + [((size // 2, chunk_rows, units), bf16)] * 6,
        50,
        out_specs=[first, first, pair] + [anywhere] * 6,
        grid=(4,),
        scratch=[pltpu.VMEM((units, width), bf16)] * 3
        + [pltpu.VMEM((rows * length, width), bf16)] * 2
        + [pltpu.VMEM((rows * length, units), bf16)]
        + [pltpu.VMEM((rows * length, wide), bf16)] * 2
        + [pltpu.VMEM((2, size // 2, chunk_rows, units), bf16)]
        + [
            pltpu.SemaphoreType.DMA((-(-units // chunk), 3)),
            pltpu.SemaphoreType.DMA((2, max(map(len, lefts)))),
            pltpu.SemaphoreType.DMA((max(rows - 1, 1), 3)),
            pltpu.SemaphoreType.DMA((3, 2, size // 2)),
        ],
    )


def halves(parts, stride, bit):
    count, rows, width = parts.shape
    pairs = parts.reshape(count // (2 * stride), 2, stride, rows, width)
    low, high = pairs[:, 0], pairs[:, 1]
    shape = (count // 2, rows, width)
    return jnp.where(bit == 0, low, high).reshape(shape), jnp.where(bit == 0, high, low).reshape(shape)


def gradient_kernel(groups, products, extra, cuts, place, *refs):
    rows = len(groups)
    extras, refs = refs[:extra], refs[extra:]
    pieces = sum(map(len, groups))
    lefts, refs = refs[:pieces], refs[pieces:]
    rights_hbm, refs = refs[: products * rows], refs[products * rows :]
    outs, refs = refs[: 2 * len(cuts)], refs[2 * len(cuts) :]
    stages, (left, right, left_sem, right_sem, out_sem) = refs[: len(cuts)], refs[len(cuts) :]
    steps = left.shape[0]
    tile = left.shape[2]
    length = right.shape[0] // rows
    cols = rights_hbm[0].shape[1]

    def left_copies(row, step):
        part = pl.ds(step * tile, tile)
        taken = sum(map(len, groups[:row]))
        copies = []
        at = row * length
        for index, lead in enumerate(groups[row]):
            source = lefts[taken + index]
            source = source if lead is None else source.at[lead]
            count = source.shape[0]
            copies.append(
                pltpu.make_async_copy(
                    source.at[:, part], left.at[step, pl.ds(at, count)], left_sem.at[step, row, index]
                )
            )
            at += count
        return copies

    def right_copy(product, row):
        index = product * rows + row
        return pltpu.make_async_copy(
            rights_hbm[index],
            right.at[pl.ds(row * length, length), pl.ds(product * cols, cols)],
            right_sem.at[index],
        )

    first = [[right_copy(product, row) for product in range(products)] + left_copies(row, 0) for row in range(rows)]
    later = [[copy for row in range(rows) for copy in left_copies(row, step)] for step in range(1, steps)]
    for group in first + later:
        for copy in group:
            copy.start()

    part_rows = tile // 2
    sending = []
    for step in range(steps):
        slot = step % 2
        sums = [None, None]
        spans = [slice(row * length, (row + 1) * length) for row in range(rows)] if step == 0 else [slice(None)]
        for span, group in zip(spans, first if step == 0 else [later[step - 1]]):
            for copy in group:
                copy.wait()
            for half in range(2):
                rows_at = slice(half * part_rows, (half + 1) * part_rows)
                part = dot_tn(left[step, span, rows_at], right[span, :])
                sums[half] = part if sums[half] is None else sums[half] + part
        for half in range(2):
            rows_at = slice(half * part_rows, (half + 1) * part_rows)
            total = sums[half]
            totals = [total[:, product * cols : (product + 1) * cols] for product in range(products)]
            if extra:
                turned_at = slice(step * tile + rows_at.start, step * tile + rows_at.stop)
                totals.append(sum(ref[0, :, turned_at].astype(f32) for ref in extras).T)
            for index, (parts, bit) in enumerate(cuts):
                chunk_rows = outs[2 * index].shape[1]
                count = part_rows // chunk_rows
                chunks = slice(half * count, (half + 1) * count)
                taken = [totals[which][:, where] for which, where in parts]
                value = taken[0] if len(taken) == 1 else jnp.concatenate(taken, axis=1)
                stages[index][slot, chunks] = value.reshape(count, chunk_rows, value.shape[1]).astype(bf16)
        for index, (parts, bit) in enumerate(cuts):
            chunk_rows = outs[2 * index].shape[1]
            mine = place[2 + bit]
            count = tile // chunk_rows // 2
            for chunk in range(count):
                low = chunk % (1 << bit)
                base = (chunk - low) * 2 + low
                for side, which in enumerate((mine, 1 - mine)):
                    copy = pltpu.make_async_copy(
                        stages[index].at[slot, base + which * (1 << bit)],
                        outs[2 * index + side].at[step * count + chunk],
                        out_sem.at[index, side, step * count + chunk],
                    )
                    copy.start()
                    sending.append(copy)
    for copy in sending:
        copy.wait()


def gradient(order, name, place, lefts, rights, cuts, extras=()):
    size = lax.axis_size("dp")
    length, cols = rights[0][0].shape
    width = lefts[0][0][0].shape[-1]
    steps = 2
    tile = width // steps
    chunk_rows = width // size
    pieces = [piece for group in lefts for piece in group]
    rows = len(lefts)
    flat = [array for group in rights for array in group]
    widths = [sum(at.stop - at.start for _, at in parts) for parts, _ in cuts]
    plan = [[lead for _, lead in group] for group in lefts]
    results = order.call(
        functools.partial(gradient_kernel, plan, len(rights), len(extras), cuts),
        name,
        (place, *extras, *[array for array, _ in pieces], *flat),
        [smem]
        + [pl.BlockSpec((1,) + extra.shape[1:], lambda *_: (0, 0, 0)) for extra in extras]
        + [anywhere] * (len(pieces) + len(flat)),
        [((size // 2, chunk_rows, w), bf16) for w in widths for _ in range(2)],
        52,
        out_specs=[anywhere] * (2 * len(widths)),
        scratch=[pltpu.VMEM((2, size // steps, chunk_rows, w), bf16) for w in widths]
        + [
            pltpu.VMEM((steps, rows * length, tile), bf16),
            pltpu.VMEM((rows * length, len(rights) * cols), bf16),
            pltpu.SemaphoreType.DMA((steps, rows, max(map(len, lefts)))),
            pltpu.SemaphoreType.DMA((len(flat),)),
            pltpu.SemaphoreType.DMA((len(cuts), 2, size // 2)),
        ],
    )
    return [results[2 * index : 2 * index + 2] for index in range(len(cuts))]


def exchange(sent, bit):
    return lax.ppermute(sent, "dp", [(i, i ^ (1 << bit)) for i in range(lax.axis_size("dp"))])


def halve_kernel(plans, place, *refs):
    count = sum(map(len, plans))
    inputs, outputs = refs[: 2 * count], refs[2 * count :]
    taken = 0
    for index, plan in enumerate(plans):
        keep_ref, send_ref = outputs[2 * index : 2 * index + 2]
        at = 0
        for stride, bit in plan:
            kept, received = inputs[2 * taken : 2 * taken + 2]
            taken += 1
            parts = kept[...].astype(f32) + received[...].astype(f32)
            keep, send = halves(parts, stride, place[2 + bit])
            cols = slice(at, at + parts.shape[2])
            keep_ref[:, :, cols] = keep.astype(bf16)
            send_ref[:, :, cols] = send.astype(bf16)
            at += parts.shape[2]


def total_kernel(*refs):
    count = 0
    while count < len(refs) and len(refs[count].shape) == 3:
        count += 1
    outs = list(refs[count:])
    for index in range(count // 2):
        total = refs[2 * index][0].astype(f32) + refs[2 * index + 1][0].astype(f32)
        at = 0
        while at < total.shape[1]:
            out = outs.pop(0)
            out[...] = total[:, at : at + out.shape[1]]
            at += out.shape[1]


class Scatter:
    def __init__(self, first, parts, last=False, widths=None):
        count = lax.axis_size("dp").bit_length() - 1
        self.bits = [first] + [bit for bit in range(count) if bit != first]
        if last:
            self.bits = self.bits[:1] + self.bits[2:] + self.bits[1:2]
        self.left = sorted(self.bits)
        self.widths = widths or [parts[0].shape[2]]
        self.send(*parts)

    def send(self, kept, sent):
        bit = self.bits.pop(0)
        self.left.remove(bit)
        self.parts = kept, exchange(sent, bit)


def halve(order, place, *groups):
    groups = [group if isinstance(group, tuple) else (group,) for group in groups]
    plans = [[(1 << scatter.left.index(scatter.bits[0]), scatter.bits[0]) for scatter in group] for group in groups]
    flat = [scatter for group in groups for scatter in group]
    shapes = [
        (group[0].parts[0].shape[0] // 2, group[0].parts[0].shape[1], sum(s.parts[0].shape[2] for s in group))
        for group in groups
    ]
    results = order.call(
        functools.partial(halve_kernel, plans),
        "halve",
        (place, *[part for scatter in flat for part in scatter.parts]),
        [smem] + [vmem] * (2 * len(flat)),
        [(shape, bf16) for shape in shapes for _ in range(2)],
        24,
    )
    for index, group in enumerate(groups):
        for other in group[1:]:
            assert group[0].left == other.left
            group[0].widths += other.widths
        group[0].send(*results[2 * index : 2 * index + 2])


def finish(order, *scatters):
    for scatter in scatters:
        assert not scatter.bits, scatter.bits
    return order.call(
        total_kernel,
        "gradient_output",
        [part for scatter in scatters for part in scatter.parts],
        [vmem] * (2 * len(scatters)),
        [
            ((scatter.parts[0].shape[1], width), f32, pltpu.HBM) for scatter in scatters for width in scatter.widths
        ],
        16,
    )


def pass_kernel(*refs):
    for keep, received, out in zip(refs[0::2], refs[1::2], refs[-(len(refs) // 3) :]):
        out[...] = (keep[...].reshape(out.shape).astype(f32) + received[...].reshape(out.shape).astype(f32)).astype(bf16)


def pass_on(order, keep, received, lead=None):
    count, width = keep.shape[0] // 2, keep.shape[1]
    second = pl.BlockSpec((count, width), lambda *_: (1, 0))
    other = second if lead is None else pl.BlockSpec((1, count, width), lambda *_: (lead, 1, 0))
    return over_y(
        order.call(pass_kernel, "pass_on", (keep, received), [second, other], [((count, width), bf16)], 8)[0]
    )


def pass_rows_kernel(*refs):
    out = refs[-1]
    for row in range(out.shape[0]):
        received = refs[2 * row + 1][...].reshape(out.shape[1:])
        out[row] = (refs[2 * row][...].astype(f32) + received.astype(f32)).astype(bf16)


def pass_rows(order, parts, lead=None):
    count, width = parts[0][0].shape[0] // 2, parts[0][0].shape[1]
    second = pl.BlockSpec((count, width), lambda *_: (1, 0))
    other = second if lead is None else pl.BlockSpec((1, count, width), lambda *_: (lead, 1, 0))
    return over_y(
        order.call(
            pass_rows_kernel,
            "pass_on",
            [array for pair in parts for array in pair],
            [second, other] * len(parts),
            [((len(parts), count, width), bf16)],
            12,
        )[0]
    )


def outproj_pass(order, keep, received):
    shape = keep.shape[1:]
    second = pl.BlockSpec((1,) + shape, lambda *_: (1, 0, 0))
    return over_y(order.call(pass_kernel, "pass_on", (keep, received), [second] * 2, [((1,) + shape, bf16)], 8)[0])


def join_kernel(bit, place, mine, received, out):
    count = mine.shape[0]
    which = place[2 + bit]
    out[pl.ds(pl.multiple_of(which * count, 16), count), :] = mine[...]
    out[pl.ds(pl.multiple_of((1 - which) * count, 16), count), :] = received[...]


def join(order, place, bit, mine, received):
    shape = (2 * mine.shape[0],) + mine.shape[1:]
    return order.call(
        functools.partial(join_kernel, bit), "join", (place, mine, received), [smem, vmem, vmem], [(shape, mine.dtype)], 8
    )[0]


def pause_kernel(out):
    out[...] = jnp.zeros_like(out)


def pause(order):
    order.call(pause_kernel, "pause", (), [], [((8, 128), f32)], 4)


def fence(order, *arrays):
    return order.call(
        lambda *_: None,
        "fence",
        arrays,
        [anywhere] * len(arrays),
        [(array.shape, array.dtype) for array in arrays],
        4,
        out_specs=[anywhere] * len(arrays),
        aliases={index: index for index in range(len(arrays))},
    )


def relay_kernel(source, target):
    target[...] = source[0] if len(source.shape) == 3 else source[...]


def relay(order, array, row=None):
    shape = array.shape if row is None else array.shape[1:]
    spec = vmem if row is None else row_of(row, array.shape)
    return order.call(relay_kernel, "relay", (array,), [spec], [(shape, array.dtype)], 8)[0]


def summed(keep, received, from_y):
    shape = keep.shape
    return sum(ref[...].reshape(shape).astype(f32) for ref in (keep, received, from_y))


def block_out_kernel(rows, *refs):
    out = refs[-1]
    for row in range(rows):
        middle, keep, received, from_y = refs[4 * row : 4 * row + 4]
        out[row] = middle[...] + summed(keep, received, from_y)


def block_output(order, middles, feeds, from_y):
    rows = len(from_y)
    count, width = from_y[0].shape
    first = pl.BlockSpec((count, width), lambda *_: (0, 0))
    other = pl.BlockSpec((1, count, width), lambda *_: (1, 0, 0))
    return order.call(
        functools.partial(block_out_kernel, rows),
        "block_output",
        [array for row in range(rows) for array in (middles[row], *feeds[row], from_y[row])],
        [vmem, first, other, vmem] * rows,
        [((rows, count, width), f32, pltpu.HBM)],
        30,
    )[0]


def input_grad_kernel(rows, from_y, inputs, gain, *refs):
    out = refs[-1]
    for row in range(rows):
        dmiddle, keep, received = refs[3 * row : 3 * row + 3]
        dnormed = summed(keep, received, from_y.at[row])
        out[row] = dmiddle[...] + norm_backward(dnormed, inputs[row].astype(f32), gain[...])


def input_gradient(order, dmiddles, inner, from_y, inputs, gain):
    rows, count, width = from_y.shape
    first = pl.BlockSpec((count, width), lambda *_: (0, 0))
    return order.call(
        functools.partial(input_grad_kernel, rows),
        "input_gradient",
        [from_y, inputs, gain] + [array for row in range(rows) for array in (dmiddles[row], *inner[row])],
        [vmem] * 3 + [vmem, first, first] * rows,
        [(from_y.shape, f32, pltpu.HBM)],
        36,
    )[0]


def small_kernel(heads, rows, buckets, place, gain, *refs):
    norms_one, norms_two, out = refs[:rows], refs[rows : 2 * rows], refs[-1]
    bands, fars = refs[2 * rows : 3 * rows], refs[3 * rows : 4 * rows]
    lines = gain.shape[1] // 128
    ones = sum(ref[...] for ref in norms_one) / gain[...]
    twos = sum(ref[...] for ref in norms_two)
    for index, vector in enumerate((ones, twos)):
        for line in range(lines):
            out[index * lines + line : index * lines + line + 1, :] = vector[:, line * 128 : (line + 1) * 128]
    side = REACH
    tiles = {}
    for key_block in range(bands[0].shape[1] // side):
        for query_block in range(bands[0].shape[2] // side):
            tiles.setdefault(key_block - 1 - query_block, []).append((key_block, query_block))
    row_at = lax.broadcasted_iota(jnp.int32, (side, side), 0)
    col_at = lax.broadcasted_iota(jnp.int32, (side, side), 1)
    lane = lax.broadcasted_iota(jnp.int32, (1, 128), 1)
    mine = lane == place[1] + 2 * place[0]
    which = lax.broadcasted_iota(jnp.int32, (buckets, 1), 0)
    for head in range(heads):
        sums = [jnp.zeros((1, side), f32) for _ in range(buckets)]
        for distance, blocks in tiles.items():
            grads = sum(
                band[head, key * side : (key + 1) * side, query * side : (query + 1) * side]
                for band in bands
                for key, query in blocks
            )
            index = bucket_of(row_at - col_at + distance * side, buckets)
            near = abs(distance) < 2
            for bucket in range(buckets):
                after = bucket >= buckets // 2
                if (near or bucket in (buckets // 2 - 1, buckets - 1)) and (distance == 0 or after == (distance > 0)):
                    sums[bucket] += jnp.sum(jnp.where(index == bucket, grads, 0.0), axis=0, keepdims=True)
        far = sum(ref[head : head + 1, :] for ref in fars)
        total = jnp.sum(jnp.concatenate(sums, axis=0), axis=1, keepdims=True)
        total = total + jnp.where(which == buckets // 2 - 1, jnp.sum(far[:, :LANES], axis=1, keepdims=True), 0.0)
        total = total + jnp.where(which == buckets - 1, jnp.sum(far[:, LANES:], axis=1, keepdims=True), 0.0)
        at = 2 * lines + head * buckets
        out[at : at + buckets, :] = jnp.where(mine, total, 0.0)


def small_gradients(order, place, heads, buckets, gain, norms_one, norms_two, bands, fars):
    lines = gain.shape[1] // 128
    rows = len(norms_one)
    return order.call(
        functools.partial(small_kernel, heads, rows, buckets),
        "small_gradients",
        (place, gain, *norms_one, *norms_two, *bands, *fars),
        [smem] + [vmem] * (1 + 4 * rows),
        [((2 * lines + heads * buckets, 128), f32)],
        16,
    )[0]


def add_kernel(*refs):
    refs[-1][...] = sum(ref[...] for ref in refs[:-1])


def add_all(order, arrays):
    return order.call(add_kernel, "small_sum", arrays, [vmem] * len(arrays), [(arrays[0].shape, f32)], 4)[0]


def small_rounds(order, vector):
    count = lax.axis_size("dp").bit_length() - 1
    sends = [over_core, over_y] + [functools.partial(exchange, bit=bit) for bit in range(count)]
    for send in sends:
        moved = send(vector)
        yield None
        vector = add_all(order, [vector, moved])
    yield vector


def per_device(
    block_input,
    out_grad,
    seg_lengths,
    norm1_gain,
    norm2_gain,
    rel_bias,
    w_query,
    w_key,
    w_value,
    w_out,
    w_gate,
    w_up,
    w_down,
):
    rows, count, width = block_input.shape
    length = 4 * count
    here = lax.axis_index("tensor")
    dp_bits = lax.axis_size("dp").bit_length() - 1
    dp_at = lax.axis_index("dp")
    place = jnp.stack([here // 2, here % 2] + [(dp_at >> bit) & 1 for bit in range(dp_bits)]).astype(jnp.int32)
    head_width = w_query.shape[1]
    heads = head_width // DK
    buckets = rel_bias.shape[0]
    gain_one = norm1_gain.astype(f32)[None]
    gain_two = norm2_gain.astype(f32)[None]
    first_head = here * heads
    weight_t = jnp.concatenate([w_query.T, w_key.T, w_value.T], axis=0)
    gate_t, up_t = w_gate.T, w_up.T

    order = Order()
    every_row = range(rows)
    last_row = rows - 1

    band, far = bias_parts(lax.dynamic_slice_in_dim(rel_bias, first_head, heads, 1), length)
    order.after(band, far, weight_t)
    first_y = over_y(block_input[0])
    input_core = over_core(block_input)
    grad_core = over_core(out_grad)
    out_core = over_core(w_out)
    input_y, input_both = [(first_y, None)], [(over_core(first_y), None)]
    grad_y, grad_both = [], []
    bits = (1, 2)
    quarter = w_out.shape[0] // 4
    out_at = (place[2 + bits[0]] + 2 * place[2 + bits[1]]) * quarter
    out_y = over_y(lax.dynamic_slice_in_dim(w_out, out_at, quarter, 0))
    order.after(input_core, grad_core, out_core)
    order.after(first_y)
    for row in range(1, rows):
        input_y.append((over_y(relay(order, block_input, row)), None))
    grad_y.append((over_y(relay(order, out_grad, 0)), None))
    out_y = (out_y, exchange(out_y, bits[0]))

    normed_one, qkvs, logsums, attended, middles = [], [], [], [], []
    normed_keeps, normed_recvs = [], []

    def second_norm(row):
        middle, normed_keep = attention_branch(
            order, attended[row], out_parts, (block_input, row), input_y[row], gain_two
        )
        middles.append(middle)
        normed_keeps.append(normed_keep)
        normed_recvs.append(over_core(normed_keep))

    def heads_arrived(row, other):
        (other,) = fence(order, other)
        attended[row][1], attended[row][3] = other, over_y(other)

    for row in every_row:
        if row == 0:
            out_y = join(order, place, bits[0], *out_y)
            out_y = (out_y, exchange(out_y, bits[1]))
        if row == 1:
            first_other = other
        normed, qkv = project(
            order, [(block_input, row), input_y[row], (input_core, row), input_both[row]], gain_one, weight_t
        )
        if row == 1:
            heads_arrived(0, first_other)
        keep, send, logsum = attention_forward(order, row, place, seg_lengths, qkv, band, far)
        normed_one.append(normed)
        qkvs.append(qkv)
        logsums.append(logsum)
        attended.append([keep, None, over_y(keep), None])
        if row == 0:
            (next_y,) = fence(order, input_y[1][0])
            input_y[1] = (next_y, None)
            input_both.append((over_core(next_y), None))
            out_y = join(order, place, bits[1], *out_y)
            out_parts = [w_out, out_core, out_y, over_core(out_y)]
            (send,) = fence(order, send)
        other = over_core(send)

    (first_grad,) = fence(order, grad_y[0][0])
    grad_y[0] = (first_grad, None)
    grad_both.append((over_core(first_grad), None))
    second_norm(0)
    heads_arrived(1, other)
    for row in range(1, rows):
        grad_y.append((over_y(relay(order, out_grad, row)), None))

    hiddens, dgates, dups, dnormed, feeds = [], [], [], [], []

    def feed(row):
        pieces = [(out_grad, row), grad_y[row], (grad_core, row), grad_both[row]]
        return feed_forward(
            order, normed_keeps[row], normed_recvs[row], (0, 1, 2, 3), pieces, gate_t, up_t, w_down
        )

    def fed(hidden, dgate, dup, dn_keep, ff_keep, sends):
        hiddens.append(hidden)
        dgates.append(dgate)
        dups.append(dup)
        received = over_core(sends)
        dnormed.append([dn_keep, received])
        feeds.append([ff_keep, received])

    fed(*feed(0))
    for row in range(1, rows):
        second_norm(row)
        grad_y[row] = (fence(order, grad_y[row][0])[0], None)
        grad_both.append((over_core(grad_y[row][0]), None))
    feeds_y = []
    dnormed[0].append(pass_on(order, *dnormed[0], lead=0))
    feeds_y.append(pass_on(order, *feeds[0], lead=1))
    lefts = [
        [piece for r in every_row for piece in ((normed_keeps[r], None), (normed_recvs[r], None))],
        [piece for r in every_row for piece in ((out_grad, r), grad_y[r], (grad_core, r), grad_both[r])],
    ]
    earlier = [(hiddens[r], dgates[r], dups[r]) for r in range(last_row)]
    dn_keep, ff_keep, sends, *parts = feed_last(order, place, lefts, earlier, gate_t, up_t, w_down, (0, 1, 0))
    received = over_core(sends)
    dnormed.append([dn_keep, received])
    feeds.append([ff_keep, received])
    down_scatter, gate_scatter = Scatter(0, parts[:2]), Scatter(1, parts[2:4], last=True)

    dmiddles, dbranches, norm2_sums, douts = [], [], [], []
    def back_to_heads(row):
        dmiddle, dbranch, norm2_sum, dout_own, dout_core, dout_y = branch_backward(
            order, row, *dnormed[row], middles[row], out_grad, gain_two, out_parts
        )
        dmiddles.append(dmiddle)
        dbranches.append(dbranch)
        norm2_sums.append(norm2_sum)
        return dout_own, dout_core, over_y(dout_y)

    def spread(dout_own, dout_core, dout_y):
        (dout_y,) = fence(order, dout_y)
        douts.append((dout_own, dout_y, over_core(jnp.stack([dout_core, dout_y[1]]))))

    dqkvs, norm1_sums, inner, band_grads, far_grads = [], [], [], [], []

    def attend_back(row):
        dqkv, dn_keep, dn_send, band_grad, far_grad, norm1_sum = attention_backward(
            order, row, place, seg_lengths, qkvs[row], douts[row], logsums[row], band, far,
            weight_t, normed_one[row],
        )
        band_grads.append(band_grad)
        far_grads.append(far_grad)
        norm1_sums.append(norm1_sum)
        dqkvs.append(dqkv)
        inner.append([dn_keep, over_core(dn_send)])

    going = back_to_heads(0)
    for row in range(1, rows):
        dnormed[row].append(pass_on(order, *dnormed[row], lead=0))
    spread(*going)
    for row in range(1, rows):
        feeds_y.append(pass_on(order, *feeds[row], lead=1))
    attend_back(0)
    up_scatter = Scatter(0, [parts[4], *fence(order, parts[5])])
    order.after(feeds_y[0])
    going = back_to_heads(1)
    order.after(inner[0][1])
    halve(order, place, down_scatter, gate_scatter)
    order.after(feeds_y[1])
    out_keep, out_send = outproj_grad(order, [part for group in attended for part in group], dbranches)
    out_recv = over_core(out_send)
    spread(*going)
    pause(order)
    out_from_y = outproj_pass(order, out_keep, out_recv)
    attend_back(1)
    small = small_gradients(
        order, place, heads, buckets, gain_one, norm1_sums, norm2_sums, band_grads, far_grads
    )
    rounds = small_rounds(order, small)
    next(rounds)
    halve(order, place, up_scatter)
    (attention_parts,) = gradient(
        order,
        "projection_gradient",
        place,
        [[(normed_one[r], None)] for r in every_row],
        [dqkvs],
        [([(0, slice(0, 3 * head_width)), (1, slice(0, head_width))], 0)],
        (out_keep, out_recv, out_from_y),
    )
    attention_scatter = Scatter(0, attention_parts, widths=[head_width] * 4)
    order.after(down_scatter.parts[1], gate_scatter.parts[1])
    next(rounds)
    inner_y = pass_rows(order, inner)
    halve(order, place, up_scatter)
    while up_scatter.bits:
        halve(order, place, up_scatter)
    block_out = block_output(order, middles, feeds, feeds_y)
    halve(order, place, attention_scatter)
    next(rounds)
    while down_scatter.bits:
        halve(order, place, down_scatter, gate_scatter)
    while attention_scatter.bits:
        halve(order, place, attention_scatter)
    next(rounds)
    input_grad = input_gradient(order, dmiddles, inner, inner_y, block_input, gain_one)
    next(rounds)
    up_out, down_out, gate_out = finish(order, up_scatter, down_scatter, gate_scatter)
    small = None
    while small is None:
        small = next(rounds)
    query_out, key_out, value_out, outproj_out = finish(order, attention_scatter)
    lines = width // 128
    bias_out = small[2 * lines :, : lax.axis_size("tensor")].reshape(heads, buckets, -1)
    bias_out = jnp.transpose(bias_out, (1, 2, 0)).reshape(rel_bias.shape)
    return (
        block_out,
        input_grad,
        small[:lines].reshape(width),
        small[lines : 2 * lines].reshape(width),
        bias_out,
        query_out,
        key_out,
        value_out,
        outproj_out.T,
        gate_out,
        up_out,
        down_out.T,
    )


def solution(mesh):
    in_specs = (
        P("dp", "tensor", None),
        P("dp", "tensor", None),
        P("dp", None),
        P(),
        P(),
        P(),
        P(None, "tensor"),
        P(None, "tensor"),
        P(None, "tensor"),
        P("tensor", None),
        P(None, "tensor"),
        P(None, "tensor"),
        P("tensor", None),
    )
    out_specs = (
        P("dp", "tensor", None),
        P("dp", "tensor", None),
        P(),
        P(),
        P(),
        P("dp", "tensor"),
        P("dp", "tensor"),
        P("dp", "tensor"),
        P("tensor", "dp"),
        P("dp", "tensor"),
        P("dp", "tensor"),
        P("tensor", "dp"),
    )
    return jax.shard_map(
        per_device, mesh=mesh, in_specs=in_specs, out_specs=out_specs, check_vma=False
    )
```

profile of v0, /device:TPU:0, one launch (start us, length us, event | category | flops | bytes accessed | tf_op | source)
XLA Modules:
  0.0 382.4 jit_solution(8049597255350270340)
XLA Ops:
  9.6 4.1 %broadcast_compare_fusion.26 = (pred[512,256]{1,0:T(8,128)(4,1)S(1)}, pred[512,256]{1,0:T(8,128)(4,1)S(1)}, pred[512,256]{1,0:T(8,128)(4,1)S(1)}, pred[512,256]{...) fusion(s32[512]{0:T(512)S(1)} %iota_add_fusion), kind=kLoop, calls=%fused_computation.48 | loop fusion | flops 7864320 | bytes 4196352 | tf_op jit(solution)/shard_map/eq | solution.py:152
  13.8 5.2 %select_select_fusion.refs_1_.refs_3_.refs_7_ = f32[3,512,256]{2,1,0:T(8,128)S(1)} fusion(f32[3]{0:T(128)S(1)} %get-tuple-element.197, f32[3]{0:T(128)S(1)} %get-tuple-element.198, f32[3]{0:T(128)S(1)} %get-tuple-element.199, f32[3]{0:T(128)S(1)} %get-tuple-element.200, f32[3]{0:T(128)S(1)} %get-tuple-element.201, f32[3]{0:T(128)S(1)} %get-tuple-element.202, ...), kind=kLoop, calls=%fused_computation.1 | loop fusion | flops 12582912 | bytes 5767552 | tf_op jit(solution)/shard_map/jit(_where)/select_n | solution.py:152
  23.3 4.4 %collective-permute-done.refs_7_.refs_1_.refs_9_ = bf16[256,1536]{1,0:T(8,128)(2,1)} collective-permute-done((bf16[256,1536]{1,0:T(8,128)(2,1)}, bf16[256,1536]{1,0:T(8,128)(2,1)}, u32[]{:S(2)}, u32[]{:S(2)}) %collective-permute-start) | collective-permute-done | bytes 786464 | tf_op jit(solution)/shard_map/ppermute | solution.py:43
  36.2 4.6 %normed_projections.2 = (bf16[1024,1536]{1,0:T(8,128)(2,1)S(1)}, bf16[1024,576]{1,0:T(8,128)(2,1)S(1)}) custom-call(bf16[2,256,1536]{2,1,0:T(8,128)(2,1)S(1)} %copy-done.8, bf16[256,1536]{1,0:T(8,128)(2,1)} %collective-permute-done.refs_7_.refs_1_.refs_9_, bf16[2,256,1536]{2,1,0:T(8,128)(2,1)} %collective-permute-done.1.refs_4_.refs_2_, ...), custom_call_target="tpu_custom_call" | custom-call | flops 9999999827968 | bytes 1024 | tf_op jit(solution)/shard_map/normed_projections/pallas_call | solution.py:84
  40.9 8.8 %attention_forward.2 = (bf16[512,192]{1,0:T(8,128)(2,1)}, bf16[512,192]{1,0:T(8,128)(2,1)}, f32[8,1024]{1,0:T(8,128)S(1)}) custom-call(s32[5]{0:T(128)S(1)} %stack.35.refs_0_, s32[2,4]{1,0:T(2,128)S(1)} %copy-done.16, bf16[1024,576]{1,0:T(8,128)(2,1)S(1)} %get-tuple-element.92.refs_2_, f32[3,512,256]{2,1,0:T(8,128)S(1)} %select_select_fusion.refs_1_.refs_3_.refs_7_, ...), custom_call_target="tpu_custom_call" | custom-call | flops 9999999827968 | bytes 1024 | tf_op jit(solution)/shard_map/attention_forward/pallas_call | solution.py:84
  54.5 4.5 %normed_projections.3 = (bf16[1024,1536]{1,0:T(8,128)(2,1)S(1)}, bf16[1024,576]{1,0:T(8,128)(2,1)S(1)}) custom-call(bf16[2,256,1536]{2,1,0:T(8,128)(2,1)S(1)} %copy-done.8, bf16[256,1536]{1,0:T(8,128)(2,1)} %fence.9.refs_3_.refs_1_.refs_9_, bf16[2,256,1536]{2,1,0:T(8,128)(2,1)} %collective-permute-done.1.refs_4_.refs_2_, ...), custom_call_target="tpu_custom_call" | custom-call | flops 9999999827968 | bytes 1024 | tf_op jit(solution)/shard_map/normed_projections/pallas_call | solution.py:84
  61.8 8.3 %attention_forward.3 = (bf16[512,192]{1,0:T(8,128)(2,1)}, bf16[512,192]{1,0:T(8,128)(2,1)}, f32[8,1024]{1,0:T(8,128)S(1)}) custom-call(s32[5]{0:T(128)S(1)} %stack.35.refs_0_, s32[2,4]{1,0:T(2,128)S(1)} %copy-done.16, bf16[1024,576]{1,0:T(8,128)(2,1)S(1)} %get-tuple-element.97.refs_2_, f32[3,512,256]{2,1,0:T(8,128)S(1)} %select_select_fusion.refs_1_.refs_3_.refs_7_, ...), custom_call_target="tpu_custom_call" | custom-call | flops 9999999827968 | bytes 1024 | tf_op jit(solution)/shard_map/attention_forward/pallas_call | solution.py:84
  72.8 5.6 %collective-permute-done.12.refs_3_ = bf16[512,192]{1,0:T(8,128)(2,1)} collective-permute-done((bf16[512,192]{1,0:T(8,128)(2,1)}, bf16[512,192]{1,0:T(8,128)(2,1)}, u32[]{:S(2)}, u32[]{:S(2)}) %collective-permute-start.12) | collective-permute-done | bytes 196640 | tf_op jit(solution)/shard_map/ppermute | solution.py:43
  78.4 5.2 %attention_branch.2 = (f32[256,1536]{1,0:T(8,128)S(1)}, bf16[512,1536]{1,0:T(8,128)(2,1)}) custom-call(bf16[512,192]{1,0:T(8,128)(2,1)} %get-tuple-element.94.refs_1_.refs_0_, bf16[512,192]{1,0:T(8,128)(2,1)} %fence.11.refs_5_.refs_1_, bf16[512,192]{1,0:T(8,128)(2,1)} %collective-permute-done.11.refs_2_, bf16[512,192]{1,0:T(8,128)(2,1)} %collective-permute-done.12.refs_3_, ...), custom_call_target="tpu_custom_call" | custom-call | flops 9999999827968 | bytes 1024 | tf_op jit(solution)/shard_map/attention_branch/pallas_call | solution.py:84
  89.5 28.5 %feed_forward.1 = (bf16[1024,992]{1,0:T(8,128)(2,1)}, bf16[1024,1024]{1,0:T(8,128)(2,1)}, bf16[1024,1024]{1,0:T(8,128)(2,1)}, bf16[512,1536]{1,0:T(8,128)(2,1)S(...) custom-call(bf16[512,1536]{1,0:T(8,128)(2,1)} %get-tuple-element.100.refs_0_.refs_1_, ...), custom_call_target="tpu_custom_call" | custom-call | flops 9999999827968 | bytes 1024 | tf_op jit(solution)/shard_map/feed_forward/pallas_call | solution.py:84
  120.8 5.2 %attention_branch.3 = (f32[256,1536]{1,0:T(8,128)S(1)}, bf16[512,1536]{1,0:T(8,128)(2,1)}) custom-call(bf16[512,192]{1,0:T(8,128)(2,1)} %get-tuple-element.98.refs_1_.refs_0_.refs_4_, bf16[512,192]{1,0:T(8,128)(2,1)} %fence.13.refs_1_.refs_5_, bf16[512,192]{1,0:T(8,128)(2,1)} %collective-permute-done.20.refs_2_.refs_6_, ...), custom_call_target="tpu_custom_call" | custom-call | flops 9999999827968 | bytes 1024 | tf_op jit(solution)/shard_map/attention_branch/pallas_call | solution.py:84
  134.2 52.1 %feed_forward_and_gradients.1 = (bf16[512,1536]{1,0:T(8,128)(2,1)}, bf16[512,1536]{1,0:T(8,128)(2,1)}, bf16[2,512,1536]{2,1,0:T(8,128)(2,1)}, bf16[4,192,992]{2,...) custom-call(s32[5]{0:T(128)S(1)} %stack.35.refs_0_, ...), custom_call_target="tpu_custom_call" | custom-call | flops 9999999827968 | bytes 1024 | tf_op jit(solution)/shard_map/feed_forward_and_gradients/pallas_call | solution.py:84
  190.9 4.6 %branch_backward.2 = (f32[256,1536]{1,0:T(8,128)S(1)}, bf16[256,1536]{1,0:T(8,128)(2,1)S(1)}, f32[1,1536]{1,0:T(1,128)S(1)}, bf16[256,192]{1,0:T(8,128)(2,1)S(1)...) custom-call(bf16[512,1536]{1,0:T(8,128)(2,1)S(1)} %copy-done.35, ...), custom_call_target="tpu_custom_call" | custom-call | flops 9999999827968 | bytes 1024 | tf_op jit(solution)/shard_map/branch_backward/pallas_call | solution.py:84
  199.7 5.2 %collective-permute-done.27.refs_0_ = bf16[2,256,192]{2,1,0:T(8,128)(2,1)} collective-permute-done((bf16[2,256,192]{2,1,0:T(8,128)(2,1)}, bf16[2,256,192]{2,1,0:T(8,128)(2,1)}, u32[]{:S(2)}, u32[]{:S(2)}) %collective-permute-start.27) | collective-permute-done | bytes 196640 | tf_op jit(solution)/shard_map/ppermute | solution.py:43
  210.1 17.4 %attention_backward.2 = (bf16[1024,576]{1,0:T(8,128)(2,1)}, bf16[512,1536]{1,0:T(8,128)(2,1)}, bf16[512,1536]{1,0:T(8,128)(2,1)}, f32[3,512,256]{2,1,0:T(8,128)}...) custom-call(s32[5]{0:T(128)S(1)} %stack.35.refs_0_, s32[2,4]{1,0:T(2,128)S(1)} %copy-done.17, bf16[1024,576]{1,0:T(8,128)(2,1)} %copy-done.53, ...), custom_call_target="tpu_custom_call" | custom-call | flops 9999999827968 | bytes 1024 | tf_op jit(solution)/shard_map/attention_backward/pallas_call | solution.py:84
  230.7 4.7 %branch_backward.3 = (f32[256,1536]{1,0:T(8,128)S(1)}, bf16[256,1536]{1,0:T(8,128)(2,1)S(1)}, f32[1,1536]{1,0:T(1,128)S(1)}, bf16[256,192]{1,0:T(8,128)(2,1)S(1)...) custom-call(bf16[512,1536]{1,0:T(8,128)(2,1)S(1)} %copy-done.31, ...), custom_call_target="tpu_custom_call" | custom-call | flops 9999999827968 | bytes 1024 | tf_op jit(solution)/shard_map/branch_backward/pallas_call | solution.py:84
  236.4 3.7 halve.6
  240.1 4.3 %outproj_gradient.1 = (bf16[2,192,1536]{2,1,0:T(8,128)(2,1)S(1)}, bf16[2,192,1536]{2,1,0:T(8,128)(2,1)}) custom-call(bf16[512,192]{1,0:T(8,128)(2,1)} %get-tuple-element.94.refs_1_.refs_0_, bf16[512,192]{1,0:T(8,128)(2,1)} %fence.11.refs_5_.refs_1_, bf16[512,192]{1,0:T(8,128)(2,1)} %collective-permute-done.11.refs_2_, ...), custom_call_target="tpu_custom_call" | custom-call | flops 9999999827968 | bytes 1024 | tf_op jit(solution)/shard_map/outproj_gradient/pallas_call | solution.py:84
  252.8 18.0 %attention_backward.3 = (bf16[1024,576]{1,0:T(8,128)(2,1)}, bf16[512,1536]{1,0:T(8,128)(2,1)}, bf16[512,1536]{1,0:T(8,128)(2,1)}, f32[3,512,256]{2,1,0:T(8,128)}...) custom-call(s32[5]{0:T(128)S(1)} %stack.35.refs_0_, s32[2,4]{1,0:T(2,128)S(1)} %copy-done.18, bf16[1024,576]{1,0:T(8,128)(2,1)} %copy-done.54, ...), custom_call_target="tpu_custom_call" | custom-call | flops 9999999827968 | bytes 1024 | tf_op jit(solution)/shard_map/attention_backward/pallas_call | solution.py:84
  281.3 11.2 %projection_gradient.1 = (bf16[4,192,768]{2,1,0:T(8,128)(2,1)}, bf16[4,192,768]{2,1,0:T(8,128)(2,1)}) custom-call(s32[5]{0:T(128)S(1)} %stack.35.refs_0_, bf16[2,192,1536]{2,1,0:T(8,128)(2,1)} %copy-done.55, bf16[2,192,1536]{2,1,0:T(8,128)(2,1)} %collective-permute-done.37.refs_1_.refs_2_, bf16[1,192,1536]{2,1,0:T(8,128)(2,1)} %collective-permute-done.41.refs_3_, ...), custom_call_target="tpu_custom_call" | custom-call | flops 9999999827968 | bytes 1024 | tf_op jit(solution)/shard_map/projection_gradient/pallas_call | solution.py:84
  305.2 4.3 %block_output.1.refs_3_ = f32[2,256,1536]{2,1,0:T(8,128)} custom-call(f32[256,1536]{1,0:T(8,128)S(1)} %copy-done.37, bf16[512,1536]{1,0:T(8,128)(2,1)S(1)} %copy-done.33, bf16[2,512,1536]{2,1,0:T(8,128)(2,1)} %collective-permute-done.18.refs_1_.refs_2_, bf16[256,1536]{1,0:T(8,128)(2,1)} %collective-permute-done.22.refs_11_.refs_3_, ...), custom_call_target="tpu_custom_call" | custom-call | flops 9999999827968 | bytes 1024 | tf_op jit(solution)/shard_map/block_output/pallas_call | solution.py:84
  309.5 14.6 %collective-permute-done.46.refs_2_ = bf16[4,192,768]{2,1,0:T(8,128)(2,1)} collective-permute-done((bf16[4,192,768]{2,1,0:T(8,128)(2,1)}, bf16[4,192,768]{2,1,0:T(8,128)(2,1)}, u32[]{:S(2)}, u32[]{:S(2)}) %collective-permute-start.46) | collective-permute-done | bytes 1179680 | tf_op jit(solution)/shard_map/ppermute | solution.py:872
  334.2 18.6 %collective-permute-done.48.refs_2_ = bf16[2,192,768]{2,1,0:T(8,128)(2,1)} collective-permute-done((bf16[2,192,768]{2,1,0:T(8,128)(2,1)}, bf16[2,192,768]{2,1,0:T(8,128)(2,1)}, u32[]{:S(2)}, u32[]{:S(2)}) %collective-permute-start.48) | collective-permute-done | bytes 589856 | tf_op jit(solution)/shard_map/ppermute | solution.py:872
  359.7 6.2 %input_gradient.1.refs_2_ = f32[2,256,1536]{2,1,0:T(8,128)} custom-call(bf16[2,256,1536]{2,1,0:T(8,128)(2,1)} %collective-permute-done.44.refs_0_, bf16[2,256,1536]{2,1,0:T(8,128)(2,1)S(1)} %copy-done.11, f32[1,1536]{1,0:T(1,128)S(1)} %reshape.774.refs_4_.refs_1_.refs_2_, f32[256,1536]{1,0:T(8,128)S(1)} %copy-done.42, bf16[512,1536]{1,0:T(8,128)(2,1)S(1)} %copy-done.44, ...), custom_call_target="tpu_custom_call" | custom-call | flops 9999999827968 | bytes 1024 | tf_op jit(solution)/shard_map/input_gradient/pallas_call | solution.py:84
  (299 shorter events, 131.5 us)
Async XLA Ops:
  0.7 27.1 %collective-permute-start.6 = (bf16[192,1536]{1,0:T(8,128)(2,1)}, bf16[192,1536]{1,0:T(8,128)(2,1)}, u32[]{:S(2)}, u32[]{:S(2)}) collective-permute-start(bf16[192,1536]{1,0:T(8,128)(2,1)} %refs_6_.3), channel_id=1, source_target_pairs={{0,1},{1,0},{2,3},{3,2},{4,5},{5,4},{6,7},{7,6},{8,9},{9,8},{10,11... | collective-permute-start | bytes 1769480 | tf_op jit(solution)/shard_map/ppermute | solution.py:47
  5.4 22.4 %collective-permute-start.1 = (bf16[2,256,1536]{2,1,0:T(8,128)(2,1)}, bf16[2,256,1536]{2,1,0:T(8,128)(2,1)}, u32[]{:S(2)}, u32[]{:S(2)}) collective-permute-start(bf16[2,256,1536]{2,1,0:T(8,128)(2,1)} %refs_1_.9), channel_id=1, source_target_pairs={{0,1},{1,0},{2,3},{3,2},{4,5},{5,4},{6,7},{7,6},{8,9},{9,8},{10,11... | collective-permute-start | bytes 4718600 | tf_op jit(solution)/shard_map/ppermute | solution.py:47
  30.6 39.5 %collective-permute-start.14 = (bf16[256,1536]{1,0:T(8,128)(2,1)}, bf16[256,1536]{1,0:T(8,128)(2,1)}, u32[]{:S(2)}, u32[]{:S(2)}) collective-permute-start(bf16[256,1536]{1,0:T(8,128)(2,1)} %relay.4.refs_3_), channel_id=1, source_target_pairs={{0,2},{2,0},{1,3},{3,1},{4,6},{6,4},{5,7},{7,5},{8,10},{10,8},{9,1... | collective-permute-start | bytes 2359304 | tf_op jit(solution)/shard_map/ppermute | solution.py:43
  49.7 23.1 %collective-permute-start.11 = (bf16[512,192]{1,0:T(8,128)(2,1)}, bf16[512,192]{1,0:T(8,128)(2,1)}, u32[]{:S(2)}, u32[]{:S(2)}) collective-permute-start(bf16[512,192]{1,0:T(8,128)(2,1)} %get-tuple-element.94.refs_1_.refs_0_), channel_id=1, source_target_pairs={{0,2},{2,0},{1,3},{3,1},{4,6},{6,4},{5,7},{7,5},{8,10},{10,8},{9,1... | collective-permute-start | bytes 589832 | tf_op jit(solution)/shard_map/ppermute | solution.py:43
  70.1 48.1 %collective-permute-start.20 = (bf16[512,192]{1,0:T(8,128)(2,1)}, bf16[512,192]{1,0:T(8,128)(2,1)}, u32[]{:S(2)}, u32[]{:S(2)}) collective-permute-start(bf16[512,192]{1,0:T(8,128)(2,1)} %get-tuple-element.98.refs_1_.refs_0_.refs_4_), channel_id=1, source_target_pairs={{0,2},{2,0},{1,3},{3,1},{4,6},{6,4},{5,7},{7,5},{8,10},{10,8},{9,1... | collective-permute-start | bytes 589832 | tf_op jit(solution)/shard_map/ppermute | solution.py:43
  84.8 33.4 %collective-permute-start.21 = (bf16[512,192]{1,0:T(8,128)(2,1)}, bf16[512,192]{1,0:T(8,128)(2,1)}, u32[]{:S(2)}, u32[]{:S(2)}) collective-permute-start(bf16[512,192]{1,0:T(8,128)(2,1)} %fence.13.refs_1_.refs_5_), channel_id=1, source_target_pairs={{0,2},{2,0},{1,3},{3,1},{4,6},{6,4},{5,7},{7,5},{8,10},{10,8},{9,1... | collective-permute-start | bytes 589832 | tf_op jit(solution)/shard_map/ppermute | solution.py:43
  86.7 39.3 %collective-permute-start.19 = (bf16[256,1536]{1,0:T(8,128)(2,1)}, bf16[256,1536]{1,0:T(8,128)(2,1)}, u32[]{:S(2)}, u32[]{:S(2)}) collective-permute-start(bf16[256,1536]{1,0:T(8,128)(2,1)} %relay.5.refs_9_), channel_id=1, source_target_pairs={{0,2},{2,0},{1,3},{3,1},{4,6},{6,4},{5,7},{7,5},{8,10},{10,8},{9,1... | collective-permute-start | bytes 2359304 | tf_op jit(solution)/shard_map/ppermute | solution.py:43
  129.9 59.6 %collective-permute-start.26 = (bf16[256,1536]{1,0:T(8,128)(2,1)}, bf16[256,1536]{1,0:T(8,128)(2,1)}, u32[]{:S(2)}, u32[]{:S(2)}) collective-permute-start(bf16[256,1536]{1,0:T(8,128)(2,1)} %pass_on.6.refs_2_), channel_id=1, source_target_pairs={{0,2},{2,0},{1,3},{3,1},{4,6},{6,4},{5,7},{7,5},{8,10},{10,8},{9,1... | collective-permute-start | bytes 2359304 | tf_op jit(solution)/shard_map/ppermute | solution.py:43
  133.2 95.6 %collective-permute-start.22 = (bf16[256,1536]{1,0:T(8,128)(2,1)}, bf16[256,1536]{1,0:T(8,128)(2,1)}, u32[]{:S(2)}, u32[]{:S(2)}) collective-permute-start(bf16[256,1536]{1,0:T(8,128)(2,1)} %pass_on.7.refs_19_), channel_id=1, source_target_pairs={{0,2},{2,0},{1,3},{3,1},{4,6},{6,4},{5,7},{7,5},{8,10},{10,8},{9,1... | collective-permute-start | bytes 2359304 | tf_op jit(solution)/shard_map/ppermute | solution.py:43
  186.3 49.1 %collective-permute-start.33 = (bf16[4,192,992]{2,1,0:T(8,128)(2,1)}, bf16[4,192,992]{2,1,0:T(8,128)(2,1)}, u32[]{:S(2)}, u32[]{:S(2)}) collective-permute-start(bf16[4,192,992]{2,1,0:T(8,128)(2,1)} %get-tuple-element.127), channel_id=1, source_target_pairs={{0,4},{4,0},{8,12},{12,8},{16,20},{20,16},{24,28},{28,24},{1,5},{5... | collective-permute-start | bytes 4571144 | tf_op jit(solution)/shard_map/ppermute | solution.py:872
  187.9 48.5 %collective-permute-start.34 = (bf16[4,192,992]{2,1,0:T(8,128)(2,1)}, bf16[4,192,992]{2,1,0:T(8,128)(2,1)}, u32[]{:S(2)}, u32[]{:S(2)}) collective-permute-start(bf16[4,192,992]{2,1,0:T(8,128)(2,1)} %get-tuple-element.129), channel_id=1, source_target_pairs={{0,8},{4,12},{8,0},{12,4},{16,24},{20,28},{24,16},{28,20},{1,9},{5... | collective-permute-start | bytes 4571144 | tf_op jit(solution)/shard_map/ppermute | solution.py:872
  198.8 30.4 %collective-permute-start.31 = (bf16[256,1536]{1,0:T(8,128)(2,1)}, bf16[256,1536]{1,0:T(8,128)(2,1)}, u32[]{:S(2)}, u32[]{:S(2)}) collective-permute-start(bf16[256,1536]{1,0:T(8,128)(2,1)} %pass_on.8.refs_1_), channel_id=1, source_target_pairs={{0,2},{2,0},{1,3},{3,1},{4,6},{6,4},{5,7},{7,5},{8,10},{10,8},{9,1... | collective-permute-start | bytes 2359304 | tf_op jit(solution)/shard_map/ppermute | solution.py:43
  209.0 31.1 %collective-permute-start.28 = (bf16[256,1536]{1,0:T(8,128)(2,1)}, bf16[256,1536]{1,0:T(8,128)(2,1)}, u32[]{:S(2)}, u32[]{:S(2)}) collective-permute-start(bf16[256,1536]{1,0:T(8,128)(2,1)} %pass_on.9.refs_11_), channel_id=1, source_target_pairs={{0,2},{2,0},{1,3},{3,1},{4,6},{6,4},{5,7},{7,5},{8,10},{10,8},{9,1... | collective-permute-start | bytes 2359304 | tf_op jit(solution)/shard_map/ppermute | solution.py:43
  229.1 47.3 %collective-permute-start.30 = (bf16[4,192,992]{2,1,0:T(8,128)(2,1)}, bf16[4,192,992]{2,1,0:T(8,128)(2,1)}, u32[]{:S(2)}, u32[]{:S(2)}) collective-permute-start(bf16[4,192,992]{2,1,0:T(8,128)(2,1)} %fence.16.refs_10_), channel_id=1, source_target_pairs={{0,4},{4,0},{8,12},{12,8},{16,20},{20,16},{24,28},{28,24},{1,5},{5... | collective-permute-start | bytes 4571144 | tf_op jit(solution)/shard_map/ppermute | solution.py:872
  246.6 45.9 %collective-permute-start.42 = (bf16[2,192,992]{2,1,0:T(8,128)(2,1)}, bf16[2,192,992]{2,1,0:T(8,128)(2,1)}, u32[]{:S(2)}, u32[]{:S(2)}) collective-permute-start(bf16[2,192,992]{2,1,0:T(8,128)(2,1)} %get-tuple-element.151), channel_id=1, source_target_pairs={{0,8},{4,12},{8,0},{12,4},{16,24},{20,28},{24,16},{28,20},{1,9},{5... | collective-permute-start | bytes 2285576 | tf_op jit(solution)/shard_map/ppermute | solution.py:872
  247.1 45.5 %collective-permute-start.43 = (bf16[2,192,992]{2,1,0:T(8,128)(2,1)}, bf16[2,192,992]{2,1,0:T(8,128)(2,1)}, u32[]{:S(2)}, u32[]{:S(2)}) collective-permute-start(bf16[2,192,992]{2,1,0:T(8,128)(2,1)} %get-tuple-element.152), channel_id=1, source_target_pairs={{0,16},{4,20},{8,24},{12,28},{16,0},{20,4},{24,8},{28,12},{1,17},{... | collective-permute-start | bytes 2285576 | tf_op jit(solution)/shard_map/ppermute | solution.py:872
  251.7 28.0 %collective-permute-start.41 = (bf16[1,192,1536]{2,1,0:T(8,128)(2,1)}, bf16[1,192,1536]{2,1,0:T(8,128)(2,1)}, u32[]{:S(2)}, u32[]{:S(2)}) collective-permute-start(bf16[1,192,1536]{2,1,0:T(8,128)(2,1)} %pass_on.10.refs_11_), channel_id=1, source_target_pairs={{0,2},{2,0},{1,3},{3,1},{4,6},{6,4},{5,7},{7,5},{8,10},{10,8},{9,1... | collective-permute-start | bytes 1769480 | tf_op jit(solution)/shard_map/ppermute | solution.py:43
  295.5 32.9 %collective-permute-start.45 = (f32[120,128]{1,0:T(8,128)}, f32[120,128]{1,0:T(8,128)}, u32[]{:S(2)}, u32[]{:S(2)}) collective-permute-start(f32[120,128]{1,0:T(8,128)} %small_sum.5.refs_4_.refs_0_), channel_id=1, source_target_pairs={{0,2},{2,0},{1,3},{3,1},{4,6},{6,4},{5,7},{7,5},{8,10},{10,8},{9,1... | collective-permute-start | bytes 184328 | tf_op jit(solution)/shard_map/ppermute | solution.py:43
  296.4 27.6 %collective-permute-start.46 = (bf16[4,192,768]{2,1,0:T(8,128)(2,1)}, bf16[4,192,768]{2,1,0:T(8,128)(2,1)}, u32[]{:S(2)}, u32[]{:S(2)}) collective-permute-start(bf16[4,192,768]{2,1,0:T(8,128)(2,1)} %get-tuple-element.154), channel_id=1, source_target_pairs={{0,4},{4,0},{8,12},{12,8},{16,20},{20,16},{24,28},{28,24},{1,5},{5... | collective-permute-start | bytes 3538952 | tf_op jit(solution)/shard_map/ppermute | solution.py:872
  300.0 57.9 %collective-permute-start.44 = (bf16[2,256,1536]{2,1,0:T(8,128)(2,1)}, bf16[2,256,1536]{2,1,0:T(8,128)(2,1)}, u32[]{:S(2)}, u32[]{:S(2)}) collective-permute-start(bf16[2,256,1536]{2,1,0:T(8,128)(2,1)} %pass_on.11.refs_3_), channel_id=1, source_target_pairs={{0,2},{2,0},{1,3},{3,1},{4,6},{6,4},{5,7},{7,5},{8,10},{10,8},{9,1... | collective-permute-start | bytes 4718600 | tf_op jit(solution)/shard_map/ppermute | solution.py:43
  303.4 67.2 %collective-permute-start.51 = (bf16[1,192,992]{2,1,0:T(8,128)(2,1)}, bf16[1,192,992]{2,1,0:T(8,128)(2,1)}, u32[]{:S(2)}, u32[]{:S(2)}) collective-permute-start(bf16[1,192,992]{2,1,0:T(8,128)(2,1)} %get-tuple-element.160), channel_id=1, source_target_pairs={{0,16},{4,20},{8,24},{12,28},{16,0},{20,4},{24,8},{28,12},{1,17},{... | collective-permute-start | bytes 1142792 | tf_op jit(solution)/shard_map/ppermute | solution.py:872
  330.0 26.2 %collective-permute-start.47 = (f32[120,128]{1,0:T(8,128)}, f32[120,128]{1,0:T(8,128)}, u32[]{:S(2)}, u32[]{:S(2)}) collective-permute-start(f32[120,128]{1,0:T(8,128)} %small_sum.6.refs_5_.refs_0_), channel_id=1, source_target_pairs={{0,4},{4,0},{8,12},{12,8},{16,20},{20,16},{24,28},{28,24},{1,5},{5... | collective-permute-start | bytes 184328 | tf_op jit(solution)/shard_map/ppermute | solution.py:872
  330.5 22.2 %collective-permute-start.48 = (bf16[2,192,768]{2,1,0:T(8,128)(2,1)}, bf16[2,192,768]{2,1,0:T(8,128)(2,1)}, u32[]{:S(2)}, u32[]{:S(2)}) collective-permute-start(bf16[2,192,768]{2,1,0:T(8,128)(2,1)} %get-tuple-element.156), channel_id=1, source_target_pairs={{0,8},{4,12},{8,0},{12,4},{16,24},{20,28},{24,16},{28,20},{1,9},{5... | collective-permute-start | bytes 1769480 | tf_op jit(solution)/shard_map/ppermute | solution.py:872
  333.6 37.0 %collective-permute-start.52 = (bf16[1,192,992]{2,1,0:T(8,128)(2,1)}, bf16[1,192,992]{2,1,0:T(8,128)(2,1)}, u32[]{:S(2)}, u32[]{:S(2)}) collective-permute-start(bf16[1,192,992]{2,1,0:T(8,128)(2,1)} %get-tuple-element.161), channel_id=1, source_target_pairs={{0,16},{4,20},{8,24},{12,28},{16,0},{20,4},{24,8},{28,12},{1,17},{... | collective-permute-start | bytes 1142792 | tf_op jit(solution)/shard_map/ppermute | solution.py:872
  (99 other events, 936.7 us)
where the time goes:
time: 388 us; the launch traced here: 382 us
  Pallas kernels  239 us (62%)
  waiting for transfers between devices  53.8 us (14%)
  starting transfers between devices  42.7 us (11%)
  local copies, waits for them, and re-layouts  31.3 us (8%)
  other arithmetic  13.6 us (4%)
    pallas_call x51, Pallas kernels, call(): pl.pallas_call(body, grid=grid, in_specs=list(in_specs) + [anywhere] * ex...  239 us
    ppermute x17, waiting for transfers between devices, exchange(): lax.ppermute(sent, 'dp', [(i, i ^ 1 << bit) for i in range(lax.axis_size(...  35 us
    unnamed x137, local copies, waits for them, and re-layouts  23 us
    ppermute x17, starting transfers between devices, exchange(): lax.ppermute(sent, 'dp', [(i, i ^ 1 << bit) for i in range(lax.axis_size(...  20.3 us
    ppermute x18, starting transfers between devices, over_y(): return lax.ppermute(array, 'tensor', across_y)  19.2 us
    ppermute x18, waiting for transfers between devices, over_y(): return lax.ppermute(array, 'tensor', across_y)  17 us
  transfers between devices with their start and end apart: 55, of which 9 were waited for; matrix products, arithmetic and copies ran while one was open for 6% of the time, Pallas kernels for 62%

commit v1 on v0

--- a/solution.py
+++ b/solution.py
@@ -958,6 +958,27 @@
     )
 
 
+def attention_total_kernel(kept, received, query, key, value, out):
+    total = kept[0].astype(f32) + received[0].astype(f32)
+    cols = query.shape[1]
+    for index, target in enumerate((query, key, value)):
+        target[...] = total[:, index * cols : (index + 1) * cols]
+    out[...] = total[:, 3 * cols :].T
+
+
+def finish_attention(order, scatter):
+    assert not scatter.bits, scatter.bits
+    rows, cols = scatter.parts[0].shape[1], scatter.widths[0]
+    return order.call(
+        attention_total_kernel,
+        "projection_outputs",
+        scatter.parts,
+        [vmem] * 2,
+        [((rows, cols), f32, pltpu.HBM)] * 3 + [((cols, rows), f32, pltpu.HBM)],
+        16,
+    )
+
+
 def pass_kernel(*refs):
     for keep, received, out in zip(refs[0::2], refs[1::2], refs[-(len(refs) // 3) :]):
         out[...] = (keep[...].reshape(out.shape).astype(f32) + received[...].reshape(out.shape).astype(f32)).astype(bf16)
@@ -1332,9 +1353,9 @@
     going = back_to_heads(0)
     for row in range(1, rows):
         dnormed[row].append(pass_on(order, *dnormed[row], lead=0))
-    spread(*going)
     for row in range(1, rows):
         feeds_y.append(pass_on(order, *feeds[row], lead=1))
+    spread(*going)
     attend_back(0)
     up_scatter = Scatter(0, [parts[4], *fence(order, parts[5])])
     order.after(feeds_y[0])
@@ -1384,7 +1405,7 @@
     small = None
     while small is None:
         small = next(rounds)
-    query_out, key_out, value_out, outproj_out = finish(order, attention_scatter)
+    query_out, key_out, value_out, outproj_out = finish_attention(order, attention_scatter)
     lines = width // 128
     bias_out = small[2 * lines :, : lax.axis_size("tensor")].reshape(heads, buckets, -1)
     bias_out = jnp.transpose(bias_out, (1, 2, 0)).reshape(rel_bias.shape)
@@ -1397,7 +1418,7 @@
         query_out,
         key_out,
         value_out,
-        outproj_out.T,
+        outproj_out,
         gate_out,
         up_out,
         down_out.T,

time: 388 us -> 413 us (1.064)
  waiting for transfers between devices: 53.8 us -> 80.3 us
    ppermute x18, waiting for transfers between devices: 17 us -> 44.4 us  [over_y(): return lax.ppermute(array, 'tensor', across_y)]
    unnamed x137 -> x136, local copies, waits for them, and re-layouts: 23 us -> 19.5 us
  transfers between devices with their start and end apart: 55 -> 55, of which waited for: 9 -> 10; matrix products, arithmetic and copies ran while one was open for 6% -> 5% of each run, Pallas kernels for 62% -> 58%
where the time goes in v1:
time: 413 us; the launch traced here: 407 us
  Pallas kernels  239 us (58%)
  waiting for transfers between devices  80.3 us (19%)
  starting transfers between devices  45.1 us (11%)
  local copies, waits for them, and re-layouts  27.7 us (7%)
  other arithmetic  12.9 us (3%)
    pallas_call x51, Pallas kernels, call(): pl.pallas_call(body, grid=grid, in_specs=list(in_specs) + [anywhere] * ex...  239 us
    ppermute x18, waiting for transfers between devices, over_y(): return lax.ppermute(array, 'tensor', across_y)  44.4 us
    ppermute x17, waiting for transfers between devices, exchange(): lax.ppermute(sent, 'dp', [(i, i ^ 1 << bit) for i in range(lax.axis_size(...  34.1 us
    ppermute x17, starting transfers between devices, exchange(): lax.ppermute(sent, 'dp', [(i, i ^ 1 << bit) for i in range(lax.axis_size(...  22.9 us
    unnamed x136, local copies, waits for them, and re-layouts  19.5 us
    ppermute x18, starting transfers between devices, over_y(): return lax.ppermute(array, 'tensor', across_y)  19.1 us
  transfers between devices with their start and end apart: 55, of which 10 were waited for; matrix products, arithmetic and copies ran while one was open for 5% of the time, Pallas kernels for 58%

profile of v1, /device:TPU:0, one launch (start us, length us, event | category | flops | bytes accessed | tf_op | source)
XLA Modules:
  0.0 406.7 jit_solution(7855658403040707442)
XLA Ops:
  9.6 4.1 %broadcast_compare_fusion.26 = (pred[512,256]{1,0:T(8,128)(4,1)S(1)}, pred[512,256]{1,0:T(8,128)(4,1)S(1)}, pred[512,256]{1,0:T(8,128)(4,1)S(1)}, pred[512,256]{...) fusion(s32[512]{0:T(512)S(1)} %iota_add_fusion), kind=kLoop, calls=%fused_computation.48 | loop fusion | flops 7864320 | bytes 4196352 | tf_op jit(solution)/shard_map/eq | solution.py:152
  13.8 5.2 %select_select_fusion.refs_1_.refs_3_.refs_7_ = f32[3,512,256]{2,1,0:T(8,128)S(1)} fusion(f32[3]{0:T(128)S(1)} %get-tuple-element.173, f32[3]{0:T(128)S(1)} %get-tuple-element.174, f32[3]{0:T(128)S(1)} %get-tuple-element.175, f32[3]{0:T(128)S(1)} %get-tuple-element.176, f32[3]{0:T(128)S(1)} %get-tuple-element.177, f32[3]{0:T(128)S(1)} %get-tuple-element.178, ...), kind=kLoop, calls=%fused_computation.1 | loop fusion | flops 12582912 | bytes 5767552 | tf_op jit(solution)/shard_map/jit(_where)/select_n | solution.py:152
  23.3 4.4 %collective-permute-done.refs_7_.refs_1_.refs_9_ = bf16[256,1536]{1,0:T(8,128)(2,1)} collective-permute-done((bf16[256,1536]{1,0:T(8,128)(2,1)}, bf16[256,1536]{1,0:T(8,128)(2,1)}, u32[]{:S(2)}, u32[]{:S(2)}) %collective-permute-start) | collective-permute-done | bytes 786464 | tf_op jit(solution)/shard_map/ppermute | solution.py:43
  36.2 4.6 %normed_projections.2 = (bf16[1024,1536]{1,0:T(8,128)(2,1)S(1)}, bf16[1024,576]{1,0:T(8,128)(2,1)S(1)}) custom-call(bf16[2,256,1536]{2,1,0:T(8,128)(2,1)S(1)} %copy-done.8, bf16[256,1536]{1,0:T(8,128)(2,1)} %collective-permute-done.refs_7_.refs_1_.refs_9_, bf16[2,256,1536]{2,1,0:T(8,128)(2,1)} %collective-permute-done.1.refs_4_.refs_2_, ...), custom_call_target="tpu_custom_call" | custom-call | flops 9999999827968 | bytes 1024 | tf_op jit(solution)/shard_map/normed_projections/pallas_call | solution.py:84
  40.9 8.8 %attention_forward.2 = (bf16[512,192]{1,0:T(8,128)(2,1)}, bf16[512,192]{1,0:T(8,128)(2,1)}, f32[8,1024]{1,0:T(8,128)S(1)}) custom-call(s32[5]{0:T(128)S(1)} %stack.35.refs_0_, s32[2,4]{1,0:T(2,128)S(1)} %copy-done.16, bf16[1024,576]{1,0:T(8,128)(2,1)S(1)} %get-tuple-element.92.refs_2_, f32[3,512,256]{2,1,0:T(8,128)S(1)} %select_select_fusion.refs_1_.refs_3_.refs_7_, ...), custom_call_target="tpu_custom_call" | custom-call | flops 9999999827968 | bytes 1024 | tf_op jit(solution)/shard_map/attention_forward/pallas_call | solution.py:84
  54.5 4.5 %normed_projections.3 = (bf16[1024,1536]{1,0:T(8,128)(2,1)S(1)}, bf16[1024,576]{1,0:T(8,128)(2,1)S(1)}) custom-call(bf16[2,256,1536]{2,1,0:T(8,128)(2,1)S(1)} %copy-done.8, bf16[256,1536]{1,0:T(8,128)(2,1)} %fence.9.refs_3_.refs_1_.refs_9_, bf16[2,256,1536]{2,1,0:T(8,128)(2,1)} %collective-permute-done.1.refs_4_.refs_2_, ...), custom_call_target="tpu_custom_call" | custom-call | flops 9999999827968 | bytes 1024 | tf_op jit(solution)/shard_map/normed_projections/pallas_call | solution.py:84
  61.8 8.3 %attention_forward.3 = (bf16[512,192]{1,0:T(8,128)(2,1)}, bf16[512,192]{1,0:T(8,128)(2,1)}, f32[8,1024]{1,0:T(8,128)S(1)}) custom-call(s32[5]{0:T(128)S(1)} %stack.35.refs_0_, s32[2,4]{1,0:T(2,128)S(1)} %copy-done.16, bf16[1024,576]{1,0:T(8,128)(2,1)S(1)} %get-tuple-element.97.refs_2_, f32[3,512,256]{2,1,0:T(8,128)S(1)} %select_select_fusion.refs_1_.refs_3_.refs_7_, ...), custom_call_target="tpu_custom_call" | custom-call | flops 9999999827968 | bytes 1024 | tf_op jit(solution)/shard_map/attention_forward/pallas_call | solution.py:84
  72.8 5.6 %collective-permute-done.12.refs_3_ = bf16[512,192]{1,0:T(8,128)(2,1)} collective-permute-done((bf16[512,192]{1,0:T(8,128)(2,1)}, bf16[512,192]{1,0:T(8,128)(2,1)}, u32[]{:S(2)}, u32[]{:S(2)}) %collective-permute-start.12) | collective-permute-done | bytes 196640 | tf_op jit(solution)/shard_map/ppermute | solution.py:43
  78.4 5.2 %attention_branch.2 = (f32[256,1536]{1,0:T(8,128)S(1)}, bf16[512,1536]{1,0:T(8,128)(2,1)}) custom-call(bf16[512,192]{1,0:T(8,128)(2,1)} %get-tuple-element.94.refs_1_.refs_0_, bf16[512,192]{1,0:T(8,128)(2,1)} %fence.11.refs_5_.refs_1_, bf16[512,192]{1,0:T(8,128)(2,1)} %collective-permute-done.11.refs_2_, bf16[512,192]{1,0:T(8,128)(2,1)} %collective-permute-done.12.refs_3_, ...), custom_call_target="tpu_custom_call" | custom-call | flops 9999999827968 | bytes 1024 | tf_op jit(solution)/shard_map/attention_branch/pallas_call | solution.py:84
  89.5 28.5 %feed_forward.1 = (bf16[1024,992]{1,0:T(8,128)(2,1)}, bf16[1024,1024]{1,0:T(8,128)(2,1)}, bf16[1024,1024]{1,0:T(8,128)(2,1)}, bf16[512,1536]{1,0:T(8,128)(2,1)S(...) custom-call(bf16[512,1536]{1,0:T(8,128)(2,1)} %get-tuple-element.100.refs_0_.refs_1_, ...), custom_call_target="tpu_custom_call" | custom-call | flops 9999999827968 | bytes 1024 | tf_op jit(solution)/shard_map/feed_forward/pallas_call | solution.py:84
  120.8 5.2 %attention_branch.3 = (f32[256,1536]{1,0:T(8,128)S(1)}, bf16[512,1536]{1,0:T(8,128)(2,1)}) custom-call(bf16[512,192]{1,0:T(8,128)(2,1)} %get-tuple-element.98.refs_1_.refs_0_.refs_4_, bf16[512,192]{1,0:T(8,128)(2,1)} %fence.13.refs_1_.refs_5_, bf16[512,192]{1,0:T(8,128)(2,1)} %collective-permute-done.20.refs_2_.refs_6_, ...), custom_call_target="tpu_custom_call" | custom-call | flops 9999999827968 | bytes 1024 | tf_op jit(solution)/shard_map/attention_branch/pallas_call | solution.py:84
  133.1 52.1 %feed_forward_and_gradients.1 = (bf16[512,1536]{1,0:T(8,128)(2,1)}, bf16[512,1536]{1,0:T(8,128)(2,1)}, bf16[2,512,1536]{2,1,0:T(8,128)(2,1)}, bf16[4,192,992]{2,...) custom-call(s32[5]{0:T(128)S(1)} %stack.35.refs_0_, ...), custom_call_target="tpu_custom_call" | custom-call | flops 9999999827968 | bytes 1024 | tf_op jit(solution)/shard_map/feed_forward_and_gradients/pallas_call | solution.py:84
  186.8 4.5 %branch_backward.2 = (f32[256,1536]{1,0:T(8,128)S(1)}, bf16[256,1536]{1,0:T(8,128)(2,1)S(1)}, f32[1,1536]{1,0:T(1,128)S(1)}, bf16[256,192]{1,0:T(8,128)(2,1)S(1)...) custom-call(bf16[512,1536]{1,0:T(8,128)(2,1)S(1)} %copy-done.34, ...), custom_call_target="tpu_custom_call" | custom-call | flops 9999999827968 | bytes 1024 | tf_op jit(solution)/shard_map/branch_backward/pallas_call | solution.py:84
  207.5 17.4 %attention_backward.2 = (bf16[1024,576]{1,0:T(8,128)(2,1)}, bf16[512,1536]{1,0:T(8,128)(2,1)}, bf16[512,1536]{1,0:T(8,128)(2,1)}, f32[3,512,256]{2,1,0:T(8,128)}...) custom-call(s32[5]{0:T(128)S(1)} %stack.35.refs_0_, s32[2,4]{1,0:T(2,128)S(1)} %copy-done.17, bf16[1024,576]{1,0:T(8,128)(2,1)} %copy-done.54, ...), custom_call_target="tpu_custom_call" | custom-call | flops 9999999827968 | bytes 1024 | tf_op jit(solution)/shard_map/attention_backward/pallas_call | solution.py:84
  226.3 29.1 %collective-permute-done.31.refs_2_ = bf16[256,1536]{1,0:T(8,128)(2,1)} collective-permute-done((bf16[256,1536]{1,0:T(8,128)(2,1)}, bf16[256,1536]{1,0:T(8,128)(2,1)}, u32[]{:S(2)}, u32[]{:S(2)}) %collective-permute-start.31) | collective-permute-done | bytes 786464 | tf_op jit(solution)/shard_map/ppermute | solution.py:43
  256.9 4.7 %branch_backward.3 = (f32[256,1536]{1,0:T(8,128)S(1)}, bf16[256,1536]{1,0:T(8,128)(2,1)S(1)}, f32[1,1536]{1,0:T(1,128)S(1)}, bf16[256,192]{1,0:T(8,128)(2,1)S(1)...) custom-call(bf16[512,1536]{1,0:T(8,128)(2,1)S(1)} %copy-done.30, ...), custom_call_target="tpu_custom_call" | custom-call | flops 9999999827968 | bytes 1024 | tf_op jit(solution)/shard_map/branch_backward/pallas_call | solution.py:84
  262.5 3.7 halve.6
  266.2 4.3 %outproj_gradient.1 = (bf16[2,192,1536]{2,1,0:T(8,128)(2,1)S(1)}, bf16[2,192,1536]{2,1,0:T(8,128)(2,1)}) custom-call(bf16[512,192]{1,0:T(8,128)(2,1)} %get-tuple-element.94.refs_1_.refs_0_, bf16[512,192]{1,0:T(8,128)(2,1)} %fence.11.refs_5_.refs_1_, bf16[512,192]{1,0:T(8,128)(2,1)} %collective-permute-done.11.refs_2_, ...), custom_call_target="tpu_custom_call" | custom-call | flops 9999999827968 | bytes 1024 | tf_op jit(solution)/shard_map/outproj_gradient/pallas_call | solution.py:84
  280.1 18.0 %attention_backward.3 = (bf16[1024,576]{1,0:T(8,128)(2,1)}, bf16[512,1536]{1,0:T(8,128)(2,1)}, bf16[512,1536]{1,0:T(8,128)(2,1)}, f32[3,512,256]{2,1,0:T(8,128)}...) custom-call(s32[5]{0:T(128)S(1)} %stack.35.refs_0_, s32[2,4]{1,0:T(2,128)S(1)} %copy-done.18, bf16[1024,576]{1,0:T(8,128)(2,1)} %copy-done.53, ...), custom_call_target="tpu_custom_call" | custom-call | flops 9999999827968 | bytes 1024 | tf_op jit(solution)/shard_map/attention_backward/pallas_call | solution.py:84
  307.5 11.2 %projection_gradient.1 = (bf16[4,192,768]{2,1,0:T(8,128)(2,1)}, bf16[4,192,768]{2,1,0:T(8,128)(2,1)}) custom-call(s32[5]{0:T(128)S(1)} %stack.35.refs_0_, bf16[2,192,1536]{2,1,0:T(8,128)(2,1)} %copy-done.55, bf16[2,192,1536]{2,1,0:T(8,128)(2,1)} %collective-permute-done.37.refs_1_.refs_2_, bf16[1,192,1536]{2,1,0:T(8,128)(2,1)} %collective-permute-done.41.refs_3_, ...), custom_call_target="tpu_custom_call" | custom-call | flops 9999999827968 | bytes 1024 | tf_op jit(solution)/shard_map/projection_gradient/pallas_call | solution.py:84
  331.3 4.3 %block_output.1.refs_3_ = f32[2,256,1536]{2,1,0:T(8,128)} custom-call(f32[256,1536]{1,0:T(8,128)S(1)} %copy-done.37, bf16[512,1536]{1,0:T(8,128)(2,1)S(1)} %copy-done.32, bf16[2,512,1536]{2,1,0:T(8,128)(2,1)} %collective-permute-done.18.refs_1_.refs_2_, bf16[256,1536]{1,0:T(8,128)(2,1)} %collective-permute-done.22.refs_11_.refs_3_, ...), custom_call_target="tpu_custom_call" | custom-call | flops 9999999827968 | bytes 1024 | tf_op jit(solution)/shard_map/block_output/pallas_call | solution.py:84
  335.6 14.6 %collective-permute-done.46.refs_2_ = bf16[4,192,768]{2,1,0:T(8,128)(2,1)} collective-permute-done((bf16[4,192,768]{2,1,0:T(8,128)(2,1)}, bf16[4,192,768]{2,1,0:T(8,128)(2,1)}, u32[]{:S(2)}, u32[]{:S(2)}) %collective-permute-start.46) | collective-permute-done | bytes 1179680 | tf_op jit(solution)/shard_map/ppermute | solution.py:872
  361.1 17.2 %collective-permute-done.48.refs_2_ = bf16[2,192,768]{2,1,0:T(8,128)(2,1)} collective-permute-done((bf16[2,192,768]{2,1,0:T(8,128)(2,1)}, bf16[2,192,768]{2,1,0:T(8,128)(2,1)}, u32[]{:S(2)}, u32[]{:S(2)}) %collective-permute-start.48) | collective-permute-done | bytes 589856 | tf_op jit(solution)/shard_map/ppermute | solution.py:872
  386.0 6.2 %input_gradient.1.refs_2_ = f32[2,256,1536]{2,1,0:T(8,128)} custom-call(bf16[2,256,1536]{2,1,0:T(8,128)(2,1)} %collective-permute-done.44.refs_0_, bf16[2,256,1536]{2,1,0:T(8,128)(2,1)S(1)} %copy-done.11, f32[1,1536]{1,0:T(1,128)S(1)} %reshape.774.refs_4_.refs_1_.refs_2_, f32[256,1536]{1,0:T(8,128)S(1)} %copy-done.42, bf16[512,1536]{1,0:T(8,128)(2,1)S(1)} %copy-done.44, ...), custom_call_target="tpu_custom_call" | custom-call | flops 9999999827968 | bytes 1024 | tf_op jit(solution)/shard_map/input_gradient/pallas_call | solution.py:84
  (298 shorter events, 133.3 us)
Async XLA Ops:
  0.7 27.1 %collective-permute-start.6 = (bf16[192,1536]{1,0:T(8,128)(2,1)}, bf16[192,1536]{1,0:T(8,128)(2,1)}, u32[]{:S(2)}, u32[]{:S(2)}) collective-permute-start(bf16[192,1536]{1,0:T(8,128)(2,1)} %refs_6_.3), channel_id=1, source_target_pairs={{0,1},{1,0},{2,3},{3,2},{4,5},{5,4},{6,7},{7,6},{8,9},{9,8},{10,11... | collective-permute-start | bytes 1769480 | tf_op jit(solution)/shard_map/ppermute | solution.py:47
  5.4 22.4 %collective-permute-start.1 = (bf16[2,256,1536]{2,1,0:T(8,128)(2,1)}, bf16[2,256,1536]{2,1,0:T(8,128)(2,1)}, u32[]{:S(2)}, u32[]{:S(2)}) collective-permute-start(bf16[2,256,1536]{2,1,0:T(8,128)(2,1)} %refs_1_.9), channel_id=1, source_target_pairs={{0,1},{1,0},{2,3},{3,2},{4,5},{5,4},{6,7},{7,6},{8,9},{9,8},{10,11... | collective-permute-start | bytes 4718600 | tf_op jit(solution)/shard_map/ppermute | solution.py:47
  30.6 39.5 %collective-permute-start.14 = (bf16[256,1536]{1,0:T(8,128)(2,1)}, bf16[256,1536]{1,0:T(8,128)(2,1)}, u32[]{:S(2)}, u32[]{:S(2)}) collective-permute-start(bf16[256,1536]{1,0:T(8,128)(2,1)} %relay.4.refs_3_), channel_id=1, source_target_pairs={{0,2},{2,0},{1,3},{3,1},{4,6},{6,4},{5,7},{7,5},{8,10},{10,8},{9,1... | collective-permute-start | bytes 2359304 | tf_op jit(solution)/shard_map/ppermute | solution.py:43
  49.7 23.1 %collective-permute-start.11 = (bf16[512,192]{1,0:T(8,128)(2,1)}, bf16[512,192]{1,0:T(8,128)(2,1)}, u32[]{:S(2)}, u32[]{:S(2)}) collective-permute-start(bf16[512,192]{1,0:T(8,128)(2,1)} %get-tuple-element.94.refs_1_.refs_0_), channel_id=1, source_target_pairs={{0,2},{2,0},{1,3},{3,1},{4,6},{6,4},{5,7},{7,5},{8,10},{10,8},{9,1... | collective-permute-start | bytes 589832 | tf_op jit(solution)/shard_map/ppermute | solution.py:43
  70.1 48.2 %collective-permute-start.20 = (bf16[512,192]{1,0:T(8,128)(2,1)}, bf16[512,192]{1,0:T(8,128)(2,1)}, u32[]{:S(2)}, u32[]{:S(2)}) collective-permute-start(bf16[512,192]{1,0:T(8,128)(2,1)} %get-tuple-element.98.refs_1_.refs_0_.refs_4_), channel_id=1, source_target_pairs={{0,2},{2,0},{1,3},{3,1},{4,6},{6,4},{5,7},{7,5},{8,10},{10,8},{9,1... | collective-permute-start | bytes 589832 | tf_op jit(solution)/shard_map/ppermute | solution.py:43
  84.8 33.4 %collective-permute-start.21 = (bf16[512,192]{1,0:T(8,128)(2,1)}, bf16[512,192]{1,0:T(8,128)(2,1)}, u32[]{:S(2)}, u32[]{:S(2)}) collective-permute-start(bf16[512,192]{1,0:T(8,128)(2,1)} %fence.13.refs_1_.refs_5_), channel_id=1, source_target_pairs={{0,2},{2,0},{1,3},{3,1},{4,6},{6,4},{5,7},{7,5},{8,10},{10,8},{9,1... | collective-permute-start | bytes 589832 | tf_op jit(solution)/shard_map/ppermute | solution.py:43
  86.7 39.3 %collective-permute-start.19 = (bf16[256,1536]{1,0:T(8,128)(2,1)}, bf16[256,1536]{1,0:T(8,128)(2,1)}, u32[]{:S(2)}, u32[]{:S(2)}) collective-permute-start(bf16[256,1536]{1,0:T(8,128)(2,1)} %relay.5.refs_9_), channel_id=1, source_target_pairs={{0,2},{2,0},{1,3},{3,1},{4,6},{6,4},{5,7},{7,5},{8,10},{10,8},{9,1... | collective-permute-start | bytes 2359304 | tf_op jit(solution)/shard_map/ppermute | solution.py:43
  129.8 55.5 %collective-permute-start.26 = (bf16[256,1536]{1,0:T(8,128)(2,1)}, bf16[256,1536]{1,0:T(8,128)(2,1)}, u32[]{:S(2)}, u32[]{:S(2)}) collective-permute-start(bf16[256,1536]{1,0:T(8,128)(2,1)} %pass_on.6.refs_2_), channel_id=1, source_target_pairs={{0,2},{2,0},{1,3},{3,1},{4,6},{6,4},{5,7},{7,5},{8,10},{10,8},{9,1... | collective-permute-start | bytes 2359304 | tf_op jit(solution)/shard_map/ppermute | solution.py:43
  201.4 24.8 %collective-permute-start.22 = (bf16[256,1536]{1,0:T(8,128)(2,1)}, bf16[256,1536]{1,0:T(8,128)(2,1)}, u32[]{:S(2)}, u32[]{:S(2)}) collective-permute-start(bf16[256,1536]{1,0:T(8,128)(2,1)} %pass_on.7.refs_19_), channel_id=1, source_target_pairs={{0,2},{2,0},{1,3},{3,1},{4,6},{6,4},{5,7},{7,5},{8,10},{10,8},{9,1... | collective-permute-start | bytes 2359304 | tf_op jit(solution)/shard_map/ppermute | solution.py:43
  202.4 59.2 %collective-permute-start.33 = (bf16[4,192,992]{2,1,0:T(8,128)(2,1)}, bf16[4,192,992]{2,1,0:T(8,128)(2,1)}, u32[]{:S(2)}, u32[]{:S(2)}) collective-permute-start(bf16[4,192,992]{2,1,0:T(8,128)(2,1)} %get-tuple-element.127), channel_id=1, source_target_pairs={{0,4},{4,0},{8,12},{12,8},{16,20},{20,16},{24,28},{28,24},{1,5},{5... | collective-permute-start | bytes 4571144 | tf_op jit(solution)/shard_map/ppermute | solution.py:872
  203.9 58.6 %collective-permute-start.34 = (bf16[4,192,992]{2,1,0:T(8,128)(2,1)}, bf16[4,192,992]{2,1,0:T(8,128)(2,1)}, u32[]{:S(2)}, u32[]{:S(2)}) collective-permute-start(bf16[4,192,992]{2,1,0:T(8,128)(2,1)} %get-tuple-element.129), channel_id=1, source_target_pairs={{0,8},{4,12},{8,0},{12,4},{16,24},{20,28},{24,16},{28,20},{1,9},{5... | collective-permute-start | bytes 4571144 | tf_op jit(solution)/shard_map/ppermute | solution.py:872
  205.5 60.7 %collective-permute-start.27 = (bf16[256,1536]{1,0:T(8,128)(2,1)}, bf16[256,1536]{1,0:T(8,128)(2,1)}, u32[]{:S(2)}, u32[]{:S(2)}) collective-permute-start(bf16[256,1536]{1,0:T(8,128)(2,1)} %pass_on.9.refs_1_), channel_id=1, source_target_pairs={{0,2},{2,0},{1,3},{3,1},{4,6},{6,4},{5,7},{7,5},{8,10},{10,8},{9,1... | collective-permute-start | bytes 2359304 | tf_op jit(solution)/shard_map/ppermute | solution.py:43
  206.6 48.8 %collective-permute-start.31 = (bf16[256,1536]{1,0:T(8,128)(2,1)}, bf16[256,1536]{1,0:T(8,128)(2,1)}, u32[]{:S(2)}, u32[]{:S(2)}) collective-permute-start(bf16[256,1536]{1,0:T(8,128)(2,1)} %pass_on.8.refs_2_), channel_id=1, source_target_pairs={{0,2},{2,0},{1,3},{3,1},{4,6},{6,4},{5,7},{7,5},{8,10},{10,8},{9,1... | collective-permute-start | bytes 2359304 | tf_op jit(solution)/shard_map/ppermute | solution.py:43
  226.2 36.3 %collective-permute-start.35 = (bf16[512,1536]{1,0:T(8,128)(2,1)}, bf16[512,1536]{1,0:T(8,128)(2,1)}, u32[]{:S(2)}, u32[]{:S(2)}) collective-permute-start(bf16[512,1536]{1,0:T(8,128)(2,1)} %get-tuple-element.131), channel_id=1, source_target_pairs={{0,1},{1,0},{2,3},{3,2},{4,5},{5,4},{6,7},{7,6},{8,9},{9,8},{10,11... | collective-permute-start | bytes 4718600 | tf_op jit(solution)/shard_map/ppermute | solution.py:47
  255.4 48.3 %collective-permute-start.30 = (bf16[4,192,992]{2,1,0:T(8,128)(2,1)}, bf16[4,192,992]{2,1,0:T(8,128)(2,1)}, u32[]{:S(2)}, u32[]{:S(2)}) collective-permute-start(bf16[4,192,992]{2,1,0:T(8,128)(2,1)} %fence.16.refs_10_), channel_id=1, source_target_pairs={{0,4},{4,0},{8,12},{12,8},{16,20},{20,16},{24,28},{28,24},{1,5},{5... | collective-permute-start | bytes 4571144 | tf_op jit(solution)/shard_map/ppermute | solution.py:872
  272.7 45.9 %collective-permute-start.42 = (bf16[2,192,992]{2,1,0:T(8,128)(2,1)}, bf16[2,192,992]{2,1,0:T(8,128)(2,1)}, u32[]{:S(2)}, u32[]{:S(2)}) collective-permute-start(bf16[2,192,992]{2,1,0:T(8,128)(2,1)} %get-tuple-element.151), channel_id=1, source_target_pairs={{0,8},{4,12},{8,0},{12,4},{16,24},{20,28},{24,16},{28,20},{1,9},{5... | collective-permute-start | bytes 2285576 | tf_op jit(solution)/shard_map/ppermute | solution.py:872
  274.3 44.4 %collective-permute-start.43 = (bf16[2,192,992]{2,1,0:T(8,128)(2,1)}, bf16[2,192,992]{2,1,0:T(8,128)(2,1)}, u32[]{:S(2)}, u32[]{:S(2)}) collective-permute-start(bf16[2,192,992]{2,1,0:T(8,128)(2,1)} %get-tuple-element.152), channel_id=1, source_target_pairs={{0,16},{4,20},{8,24},{12,28},{16,0},{20,4},{24,8},{28,12},{1,17},{... | collective-permute-start | bytes 2285576 | tf_op jit(solution)/shard_map/ppermute | solution.py:872
  279.0 28.0 %collective-permute-start.41 = (bf16[1,192,1536]{2,1,0:T(8,128)(2,1)}, bf16[1,192,1536]{2,1,0:T(8,128)(2,1)}, u32[]{:S(2)}, u32[]{:S(2)}) collective-permute-start(bf16[1,192,1536]{2,1,0:T(8,128)(2,1)} %pass_on.10.refs_11_), channel_id=1, source_target_pairs={{0,2},{2,0},{1,3},{3,1},{4,6},{6,4},{5,7},{7,5},{8,10},{10,8},{9,1... | collective-permute-start | bytes 1769480 | tf_op jit(solution)/shard_map/ppermute | solution.py:43
  321.6 32.9 %collective-permute-start.45 = (f32[120,128]{1,0:T(8,128)}, f32[120,128]{1,0:T(8,128)}, u32[]{:S(2)}, u32[]{:S(2)}) collective-permute-start(f32[120,128]{1,0:T(8,128)} %small_sum.5.refs_4_.refs_0_), channel_id=1, source_target_pairs={{0,2},{2,0},{1,3},{3,1},{4,6},{6,4},{5,7},{7,5},{8,10},{10,8},{9,1... | collective-permute-start | bytes 184328 | tf_op jit(solution)/shard_map/ppermute | solution.py:43
  322.5 27.6 %collective-permute-start.46 = (bf16[4,192,768]{2,1,0:T(8,128)(2,1)}, bf16[4,192,768]{2,1,0:T(8,128)(2,1)}, u32[]{:S(2)}, u32[]{:S(2)}) collective-permute-start(bf16[4,192,768]{2,1,0:T(8,128)(2,1)} %get-tuple-element.154), channel_id=1, source_target_pairs={{0,4},{4,0},{8,12},{12,8},{16,20},{20,16},{24,28},{28,24},{1,5},{5... | collective-permute-start | bytes 3538952 | tf_op jit(solution)/shard_map/ppermute | solution.py:872
  326.1 57.4 %collective-permute-start.44 = (bf16[2,256,1536]{2,1,0:T(8,128)(2,1)}, bf16[2,256,1536]{2,1,0:T(8,128)(2,1)}, u32[]{:S(2)}, u32[]{:S(2)}) collective-permute-start(bf16[2,256,1536]{2,1,0:T(8,128)(2,1)} %pass_on.11.refs_3_), channel_id=1, source_target_pairs={{0,2},{2,0},{1,3},{3,1},{4,6},{6,4},{5,7},{7,5},{8,10},{10,8},{9,1... | collective-permute-start | bytes 4718600 | tf_op jit(solution)/shard_map/ppermute | solution.py:43
  329.5 66.7 %collective-permute-start.51 = (bf16[1,192,992]{2,1,0:T(8,128)(2,1)}, bf16[1,192,992]{2,1,0:T(8,128)(2,1)}, u32[]{:S(2)}, u32[]{:S(2)}) collective-permute-start(bf16[1,192,992]{2,1,0:T(8,128)(2,1)} %get-tuple-element.160), channel_id=1, source_target_pairs={{0,16},{4,20},{8,24},{12,28},{16,0},{20,4},{24,8},{28,12},{1,17},{... | collective-permute-start | bytes 1142792 | tf_op jit(solution)/shard_map/ppermute | solution.py:872
  356.1 25.7 %collective-permute-start.47 = (f32[120,128]{1,0:T(8,128)}, f32[120,128]{1,0:T(8,128)}, u32[]{:S(2)}, u32[]{:S(2)}) collective-permute-start(f32[120,128]{1,0:T(8,128)} %small_sum.6.refs_5_.refs_0_), channel_id=1, source_target_pairs={{0,4},{4,0},{8,12},{12,8},{16,20},{20,16},{24,28},{28,24},{1,5},{5... | collective-permute-start | bytes 184328 | tf_op jit(solution)/shard_map/ppermute | solution.py:872
  360.8 35.4 %collective-permute-start.52 = (bf16[1,192,992]{2,1,0:T(8,128)(2,1)}, bf16[1,192,992]{2,1,0:T(8,128)(2,1)}, u32[]{:S(2)}, u32[]{:S(2)}) collective-permute-start(bf16[1,192,992]{2,1,0:T(8,128)(2,1)} %get-tuple-element.161), channel_id=1, source_target_pairs={{0,16},{4,20},{8,24},{12,28},{16,0},{20,4},{24,8},{28,12},{1,17},{... | collective-permute-start | bytes 1142792 | tf_op jit(solution)/shard_map/ppermute | solution.py:872
  (99 other events, 1013.1 us)
